TPU v7x, 256 devices: a whole 4x4x8 slice. The times are simulated.
256 devices in a mesh: row: 16 (over y, z_lo, core), col: 16 (over x, z_hi).
Axes of the slice: x: 4, y: 4, z: 8 (z_hi: 4, z_lo: 2; z = z_hi * 2 + z_lo), core: 2. Of those that a mesh axis runs over, the one named last changes fastest.
Arguments:
- node_features: bfloat16 [65536, 512], P('col', 'row'), may hold values from -6 to 6
- layer_weight: bfloat16 [512, 512], replicated, may hold values from -0.25 to 0.25
- tile_values: bfloat16 [16, 16, 96, 128, 128], P('row', 'col')
- tile_coords: int32 [16, 16, 96, 2], P('row', 'col'), may hold values from 0 to 31, as said below
- tile_count: int32 [16, 16], P('row', 'col'), may hold values from 32 to 96, as said below
- cotangent: bfloat16 [65536, 512], P(('row', 'col')), may hold values from -6 to 6
Outputs:
- hidden: bfloat16 [65536, 512], P(('row', 'col'))
- grad_weight: float32 [512, 512], replicated
- grad_features: bfloat16 [65536, 512], P('col', 'row')
Inputs may be any that keep to these rules, and one draw needn't show every extreme that they name: `tile_coords`: entry 0 of a slot is its destination tile within the destination block, below 32; entry 1 its source tile within the source block, below 32; the slots of one block pair name distinct positions. `tile_count`: slots at or beyond the count hold arbitrary tiles that are not part of the adjacency.
All inputs are finite; a program needn't handle non-finite values.
Results may differ from a plain program's by a relative error of at most 0.0054.
Values may be sent and summed in bfloat16 or wider, within the bound.
A program may use at most 128 MiB of HBM per device.

v0:
```python
import math

import jax
import jax.numpy as jnp
from jax import lax
from jax.sharding import PartitionSpec as P


def tile_sweep(
    tile_groups, pick_groups, place_groups, live_groups, source_tiles, out_tiles, backward_dir
):
    tile_size = source_tiles.shape[1]
    width = source_tiles.shape[2]

    def one_turn(totals, inputs):
        block_tiles, picked, placed, live_block = inputs
        gathered_rows = source_tiles[picked]
        if backward_dir:
            product = jnp.einsum(
                "tab,tak->tbk", block_tiles, gathered_rows, preferred_element_type=jnp.float32
            )
        else:
            product = jnp.einsum(
                "tab,tbk->tak", block_tiles, gathered_rows, preferred_element_type=jnp.float32
            )
        product = jnp.where(live_block[:, None, None], product, jnp.float32(0.0))
        return (totals.at[placed].add(product), None)

    start_totals = jnp.zeros((out_tiles, tile_size, width), jnp.float32)
    totals, unused = lax.scan(
        one_turn, start_totals, (tile_groups, pick_groups, place_groups, live_groups)
    )
    return totals


def body(node_features, layer_weight, tile_values, tile_coords, tile_count, cotangent):
    slots = tile_values.shape[2]
    tile_size = tile_values.shape[3]
    width = layer_weight.shape[0]
    tiles = tile_values[0, 0]
    coords = tile_coords[0, 0]
    live_count = tile_count[0, 0]
    block_r = cotangent.shape[0] * lax.axis_size("col")
    block_c = node_features.shape[0]
    dest_tiles = block_r // tile_size
    source_count = block_c // tile_size
    group_size = math.gcd(slots, 16)
    group_count = slots // group_size
    is_live = jnp.arange(slots) < live_count
    tile_groups = tiles.reshape(group_count, group_size, tile_size, tile_size)
    dest_picks = coords[:, 0].reshape(group_count, group_size)
    source_picks = coords[:, 1].reshape(group_count, group_size)
    live_groups = is_live.reshape(group_count, group_size)
    shard_piece = lax.all_gather(node_features, "row", axis=1, tiled=True)
    piece_width = shard_piece.shape[1]
    source_tiles = shard_piece.reshape(source_count, tile_size, piece_width)
    totals = tile_sweep(
        tile_groups, source_picks, dest_picks, live_groups, source_tiles, dest_tiles, False
    )
    partial_value = totals.reshape(block_r, piece_width)
    aggregated = lax.psum_scatter(partial_value, "col", scatter_dimension=0, tiled=True).astype(
        jnp.bfloat16
    )
    pre_act = jnp.dot(aggregated, layer_weight, preferred_element_type=jnp.float32)
    hidden = jax.nn.elu(pre_act).astype(jnp.bfloat16)
    slope = jnp.where(pre_act > 0, jnp.float32(1.0), jnp.exp(jnp.minimum(pre_act, 0.0)))
    grad_pre = (cotangent.astype(jnp.float32) * slope).astype(jnp.bfloat16)
    weight_term = jnp.einsum("nf,ng->fg", aggregated, grad_pre, preferred_element_type=jnp.float32)
    grad_weight = lax.psum(weight_term, ("row", "col"))
    grad_agg = jnp.einsum(
        "ng,fg->nf", grad_pre, layer_weight, preferred_element_type=jnp.float32
    ).astype(jnp.bfloat16)
    block_grads = lax.all_gather(grad_agg, "col", axis=0, tiled=True)
    dest_rows = block_grads.reshape(dest_tiles, tile_size, width)
    back = tile_sweep(
        tile_groups, dest_picks, source_picks, live_groups, dest_rows, source_count, True
    )
    back = back.reshape(block_c, width)
    grad_features = lax.psum_scatter(back, "row", scatter_dimension=1, tiled=True).astype(
        jnp.bfloat16
    )
    return (hidden, grad_weight, grad_features)


def solution(mesh):
    in_specs = (
        P("col", "row"),
        P(),
        P("row", "col", None, None, None),
        P("row", "col", None, None),
        P("row", "col"),
        P(("row", "col"), None),
    )
    out_specs = (P(("row", "col"), None), P(), P("col", "row"))
    return jax.shard_map(body, mesh=mesh, in_specs=in_specs, out_specs=out_specs, check_vma=False)
```

profile of v0, /device:TPU:2, one launch (start us, length us, event | category | flops | bytes accessed | tf_op | source)
XLA Modules:
  0.0 839.8 jit_solution(17657270045609200235)
XLA Ops:
  9.5 43.3 %all-gather.3.cloned.1.call-done = bf16[4096,512]{0,1:T(8,128)(2,1)} async-done(((bf16[4096,32]{0,1:T(8,128)(2,1)}), bf16[4096,512]{0,1:T(8,128)(2,1)}) %all-gather.3.cloned.1.call-update) | async-done | bytes 4194320 | tf_op jit(solution)/shard_map/all_gather | solution.py:54
  52.8 6.5 copy.10
  59.3 4.3 broadcast.77.clone
  63.6 96.9 %while.20 = (s32[]{:T(128)}, f32[32,128,512]{2,1,0:T(8,128)}, s32[6,16]{1,0:T(8,128)S(1)}, pred[6,16]{1,0:T(8,128)(4,1)S(1)}, bf16[6,16,128,128]{3,2,1,0:T(8,128...) while((s32[]{:T(128)}, f32[32,128,512]{2,1,0:T(8,128)}, s32[6,16]{1,0:T(8,128)S(1)}, ...), condition=%wide.region_2.3_spmd, body=%wide.region_0.2_spmd.sunk | while | flops 270533728 | bytes 23597656 | solution.py:30
  70.2 9.7 %scatter_fusion = f32[32,128,512]{2,1,0:T(8,128)} fusion(f32[32,128,512]{2,1,0:T(8,128)} %get-tuple-element.225, s32[16]{0:T(128)S(1)} %get-tuple-element.205, f32[16,128,512]{2,1,0:T(8,128)} %convolution_select_fusion.4), kind=kCustom, calls=%fused_computation.2.clone.1 | custom fusion | flops 1048576 | bytes 12582976 | tf_op jit(solution)/shard_map/while/body/eval_jaxpr/scatter-add | solution.py:27
  86.4 9.6 %scatter_fusion = f32[32,128,512]{2,1,0:T(8,128)} fusion(f32[32,128,512]{2,1,0:T(8,128)} %get-tuple-element.225, s32[16]{0:T(128)S(1)} %get-tuple-element.205, f32[16,128,512]{2,1,0:T(8,128)} %convolution_select_fusion.4), kind=kCustom, calls=%fused_computation.2.clone.1 | custom fusion | flops 1048576 | bytes 12582976 | tf_op jit(solution)/shard_map/while/body/eval_jaxpr/scatter-add | solution.py:27
  102.6 9.6 %scatter_fusion = f32[32,128,512]{2,1,0:T(8,128)} fusion(f32[32,128,512]{2,1,0:T(8,128)} %get-tuple-element.225, s32[16]{0:T(128)S(1)} %get-tuple-element.205, f32[16,128,512]{2,1,0:T(8,128)} %convolution_select_fusion.4), kind=kCustom, calls=%fused_computation.2.clone.1 | custom fusion | flops 1048576 | bytes 12582976 | tf_op jit(solution)/shard_map/while/body/eval_jaxpr/scatter-add | solution.py:27
  118.8 9.5 %scatter_fusion = f32[32,128,512]{2,1,0:T(8,128)} fusion(f32[32,128,512]{2,1,0:T(8,128)} %get-tuple-element.225, s32[16]{0:T(128)S(1)} %get-tuple-element.205, f32[16,128,512]{2,1,0:T(8,128)} %convolution_select_fusion.4), kind=kCustom, calls=%fused_computation.2.clone.1 | custom fusion | flops 1048576 | bytes 12582976 | tf_op jit(solution)/shard_map/while/body/eval_jaxpr/scatter-add | solution.py:27
  134.9 9.4 %scatter_fusion = f32[32,128,512]{2,1,0:T(8,128)} fusion(f32[32,128,512]{2,1,0:T(8,128)} %get-tuple-element.225, s32[16]{0:T(128)S(1)} %get-tuple-element.205, f32[16,128,512]{2,1,0:T(8,128)} %convolution_select_fusion.4), kind=kCustom, calls=%fused_computation.2.clone.1 | custom fusion | flops 1048576 | bytes 12582976 | tf_op jit(solution)/shard_map/while/body/eval_jaxpr/scatter-add | solution.py:27
  150.9 9.6 %scatter_fusion = f32[32,128,512]{2,1,0:T(8,128)} fusion(f32[32,128,512]{2,1,0:T(8,128)} %get-tuple-element.225, s32[16]{0:T(128)S(1)} %get-tuple-element.205, f32[16,128,512]{2,1,0:T(8,128)} %convolution_select_fusion.4), kind=kCustom, calls=%fused_computation.2.clone.1 | custom fusion | flops 1048576 | bytes 12582976 | tf_op jit(solution)/shard_map/while/body/eval_jaxpr/scatter-add | solution.py:27
  160.5 121.4 %reduce-scatter.3.cloned.1.call-done = f32[256,512]{1,0:T(8,128)} async-done(((f32[4096,512]{1,0:T(8,128)}), f32[256,512]{1,0:T(8,128)}) %reduce-scatter.3.cloned.1.call-update) | async-done | bytes 524304 | tf_op jit(solution)/shard_map/reduce_scatter | solution.py:61
  285.3 4.7 copy.9
  290.0 70.0 %all-gather.5.cloned.1.call-done = bf16[4096,512]{1,0:T(8,128)(2,1)} async-done(((bf16[256,512]{1,0:T(8,128)(2,1)}), bf16[4096,512]{1,0:T(8,128)(2,1)}) %all-gather.5.cloned.1.call-update) | async-done | bytes 4194320 | tf_op jit(solution)/shard_map/all_gather | solution.py:73
  360.0 4.3 broadcast.77
  364.3 97.3 %while.21 = (s32[]{:T(128)}, f32[32,128,512]{2,1,0:T(8,128)}, s32[6,16]{1,0:T(8,128)S(1)}, pred[6,16]{1,0:T(8,128)(4,1)S(1)}, bf16[6,16,128,128]{2,3,1,0:T(8,128...) while((s32[]{:T(128)}, f32[32,128,512]{2,1,0:T(8,128)}, s32[6,16]{1,0:T(8,128)S(1)}, ...), condition=%wide.region_7.8_spmd, body=%wide.region_5.7_spmd.sunk | while | flops 270533728 | bytes 23597656 | solution.py:30
  370.9 9.5 %scatter_fusion.1 = f32[32,128,512]{2,1,0:T(8,128)} fusion(f32[32,128,512]{2,1,0:T(8,128)} %get-tuple-element.249, s32[16]{0:T(128)S(1)} %get-tuple-element.214, f32[16,128,512]{2,1,0:T(8,128)} %convolution_select_fusion.5), kind=kCustom, calls=%fused_computation.3.clone.1 | custom fusion | flops 1048576 | bytes 12582976 | tf_op jit(solution)/shard_map/while/body/eval_jaxpr/scatter-add | solution.py:27
  387.0 9.6 %scatter_fusion.1 = f32[32,128,512]{2,1,0:T(8,128)} fusion(f32[32,128,512]{2,1,0:T(8,128)} %get-tuple-element.249, s32[16]{0:T(128)S(1)} %get-tuple-element.214, f32[16,128,512]{2,1,0:T(8,128)} %convolution_select_fusion.5), kind=kCustom, calls=%fused_computation.3.clone.1 | custom fusion | flops 1048576 | bytes 12582976 | tf_op jit(solution)/shard_map/while/body/eval_jaxpr/scatter-add | solution.py:27
  403.3 9.5 %scatter_fusion.1 = f32[32,128,512]{2,1,0:T(8,128)} fusion(f32[32,128,512]{2,1,0:T(8,128)} %get-tuple-element.249, s32[16]{0:T(128)S(1)} %get-tuple-element.214, f32[16,128,512]{2,1,0:T(8,128)} %convolution_select_fusion.5), kind=kCustom, calls=%fused_computation.3.clone.1 | custom fusion | flops 1048576 | bytes 12582976 | tf_op jit(solution)/shard_map/while/body/eval_jaxpr/scatter-add | solution.py:27
  419.4 9.7 %scatter_fusion.1 = f32[32,128,512]{2,1,0:T(8,128)} fusion(f32[32,128,512]{2,1,0:T(8,128)} %get-tuple-element.249, s32[16]{0:T(128)S(1)} %get-tuple-element.214, f32[16,128,512]{2,1,0:T(8,128)} %convolution_select_fusion.5), kind=kCustom, calls=%fused_computation.3.clone.1 | custom fusion | flops 1048576 | bytes 12582976 | tf_op jit(solution)/shard_map/while/body/eval_jaxpr/scatter-add | solution.py:27
  435.7 9.6 %scatter_fusion.1 = f32[32,128,512]{2,1,0:T(8,128)} fusion(f32[32,128,512]{2,1,0:T(8,128)} %get-tuple-element.249, s32[16]{0:T(128)S(1)} %get-tuple-element.214, f32[16,128,512]{2,1,0:T(8,128)} %convolution_select_fusion.5), kind=kCustom, calls=%fused_computation.3.clone.1 | custom fusion | flops 1048576 | bytes 12582976 | tf_op jit(solution)/shard_map/while/body/eval_jaxpr/scatter-add | solution.py:27
  451.9 9.7 %scatter_fusion.1 = f32[32,128,512]{2,1,0:T(8,128)} fusion(f32[32,128,512]{2,1,0:T(8,128)} %get-tuple-element.249, s32[16]{0:T(128)S(1)} %get-tuple-element.214, f32[16,128,512]{2,1,0:T(8,128)} %convolution_select_fusion.5), kind=kCustom, calls=%fused_computation.3.clone.1 | custom fusion | flops 1048576 | bytes 12582976 | tf_op jit(solution)/shard_map/while/body/eval_jaxpr/scatter-add | solution.py:27
  461.6 8.9 %copy.14 = f32[4096,512]{0,1:T(8,128)} copy(f32[4096,512]{1,0:T(8,128)} %bitcast.75) | data formatting | bytes 16777216 | tf_op jit(solution)/shard_map/reshape | solution.py:78
  473.0 97.8 %reduce-scatter.5.cloned.1.call-done = f32[4096,32]{0,1:T(8,128)} async-done(((f32[4096,512]{0,1:T(8,128)}), f32[4096,32]{0,1:T(8,128)}) %reduce-scatter.5.cloned.1.call-update) | async-done | bytes 524304 | tf_op jit(solution)/shard_map/reduce_scatter | solution.py:79
  572.5 258.5 %all-reduce.2.cloned.1.call-done = f32[512,512]{1,0:T(8,128)} async-done(((f32[512,512]{1,0:T(8,128)}), f32[512,512]{1,0:T(8,128)}) %all-reduce.2.cloned.1.call-update) | async-done | bytes 1048592 | tf_op jit(solution)/shard_map/psum | solution.py:69
  (85 shorter events, 90.5 us)
Async XLA Ops:
  7.2 274.8 %copy-start = (bf16[512,512]{1,0:T(8,128)(2,1)S(1)}, bf16[512,512]{1,0:T(8,128)(2,1)}, u32[]{:S(2)}) copy-start(bf16[512,512]{1,0:T(8,128)(2,1)} %param.11) | copy-start | bytes 1572868
  7.2 45.6 %all-gather.3.cloned.1.call-start = ((), (), s32[]{:S(2)}) async-start(), calls=%async_computation.2 | async-start | bytes 4456448 | tf_op jit(solution)/shard_map/all_gather | solution.py:54
  7.9 274.1 %reduce-scatter.3.cloned.1.call-start = ((), (), s32[]{:S(2)}) async-start(), calls=%async_computation.3 | async-start | bytes 8912896 | tf_op jit(solution)/shard_map/reduce_scatter | solution.py:61
  160.5 123.7 %copy-start.2 = (bf16[256,512]{1,0:T(8,128)(2,1)S(1)}, bf16[256,512]{1,0:T(8,128)(2,1)}, u32[]{:S(2)}) copy-start(bf16[256,512]{1,0:T(8,128)(2,1)} %param.15) | copy-start | bytes 786436
  160.5 199.5 %all-gather.5.cloned.1.call-start = ((), (), s32[]{:S(2)}) async-start(), calls=%async_computation.5 | async-start | bytes 4456448 | tf_op jit(solution)/shard_map/all_gather | solution.py:73
  285.2 285.5 %reduce-scatter.5.cloned.1.call-start = ((), (), s32[]{:S(2)}) async-start(), calls=%async_computation.6 | async-start | bytes 8912896 | tf_op jit(solution)/shard_map/reduce_scatter | solution.py:79
  470.5 1.0 copy-start.1
  470.6 360.5 %all-reduce.2.cloned.1.call-start = ((), (), s32[]{:S(2)}) async-start(), calls=%async_computation.4 | async-start | bytes 2097152 | tf_op jit(solution)/shard_map/psum | solution.py:69
Sparse Core Ops, SparseCore 0:
  9.9 42.9 all-gather.2
  160.6 121.3 reduce-scatter.2
  285.4 74.6 all-gather.4
  470.7 100.0 reduce-scatter.4
  576.6 254.3 all-reduce.1
where the time goes:
time: 842 us; the launch traced here: 840 us
  waiting for transfers between devices  592 us (70%)
  other arithmetic  117 us (14%)
  local copies, waits for them, and re-layouts  67.4 us (8%)
  matrix products  49 us (6%)
  between operations  14.4 us (2%)
    psum x1, waiting for transfers between devices, body(): grad_weight = lax.psum(weight_term, ('row', 'col'))  258 us
    reduce_scatter x1, waiting for transfers between devices, body(): lax.psum_scatter(partial_value, 'col', scatter_dimension=0, tiled=True)  121 us
    scatter-add x12, other arithmetic, one_turn(): return (totals.at[placed].add(product), None)  115 us
    reduce_scatter x1, waiting for transfers between devices, body(): lax.psum_scatter(back, 'row', scatter_dimension=1, tiled=True)  97.8 us
    all_gather x1, waiting for transfers between devices, body(): block_grads = lax.all_gather(grad_agg, 'col', axis=0, tiled=True)  70 us
    all_gather x1, waiting for transfers between devices, body(): shard_piece = lax.all_gather(node_features, 'row', axis=1, tiled=True)  43.3 us
    gather x12, local copies, waits for them, and re-layouts, one_turn(): gathered_rows = source_tiles[picked]  34.4 us
    dot_general x6, matrix products, one_turn(): jnp.einsum('tab,tak->tbk', block_tiles, gathered_rows, preferred_element_...  22.3 us
  transfers between devices with their start and end apart: 5, of which 5 were waited for; matrix products, arithmetic and copies ran while one was open for 1% of the time, Pallas kernels for 0%

commit v1 on v0

v1 whole, which is shorter than its diff:
```python
import jax
import jax.numpy as jnp
from jax import lax
from jax.experimental import pallas as pl
from jax.experimental.pallas import tpu as pltpu
from jax.sharding import PartitionSpec as P

MESH = pl.DeviceIdType.MESH
BF16 = jnp.bfloat16
F32 = jnp.float32

SLOTS = 96
TILES = 32
TILE = 128
WIDTH = 512
CHUNK = 256
UNROLL = 4
WIRES = 144

NT = (((1,), (1,)), ((), ()))
NN = (((1,), (0,)), ((), ()))
TN = (((0,), (0,)), ((), ()))


def dot(a, b, dims):
    return lax.dot_general(a, b, dims, preferred_element_type=F32)


def order_table(main, other, live):
    index = jnp.arange(SLOTS, dtype=jnp.int32)
    key = jnp.where(live, main * 64 + other, 4096 + index)
    before = key[None, :] < key[:, None]
    rank = jnp.sum(before, axis=1, dtype=jnp.int32)
    same = before & live[None, :] & (main[None, :] == main[:, None])
    first = jnp.logical_not(jnp.any(same, axis=1)).astype(jnp.int32)
    places = rank[None, :] == index[:, None]
    facts = jnp.stack([index, jnp.where(live, other, 0), first])
    ordered = jnp.sum(jnp.where(places[None], facts[:, None, :], 0), axis=2, dtype=jnp.int32)
    upto = jnp.sum(live[None, :] & (main[None, :] <= index[:, None]), axis=1, dtype=jnp.int32)
    count = jnp.sum(live[None, :] & (main[None, :] == index[:, None]), axis=1, dtype=jnp.int32)
    last = jnp.maximum(upto - 1, 0)
    return jnp.concatenate([ordered, last[None], count[None]])


def kernel(
    table, xt, tiles, weight, cot, hid, gw, gft,
    xg0, xg1, run, ys, yown, xrl, xrr, xinl, xinr, zs, zrl, zrr, zinl, zinr,
    aggt, gpre, gg0, gg1, bown, bsend, cin, yb, yrl, yrr, yinl, yinr, zout, zpin,
    gsum, gout, rin_c, rin_z, rin_y, rin_x, rin_h, send_sem, recv_sem,
):
    xg, gg = (xg0, xg1), (gg0, gg1)
    r = lax.axis_index("row")
    c = lax.axis_index("col")
    y, zl, core = r // 4, (r // 2) % 2, r % 2
    x, zh = c // 4, c % 4

    def turn(v, by):
        return (v + by) % 4

    def at_y(by):
        return (turn(y, by) * 4 + r % 4, c)

    def at_x(by):
        return (r, turn(x, by) * 4 + zh)

    def at_h(by):
        return (r, x * 4 + turn(zh, by))

    at_z = (r + 2 - 4 * zl, c)
    at_core = (r + 1 - 2 * core, c)

    barrier = pltpu.get_barrier_semaphore()
    peers = [at_z, at_core] + [f(by) for f in (at_y, at_x, at_h) for by in (1, 2, 3)]
    for peer in peers:
        pl.semaphore_signal(barrier, inc=1, device_id=peer, device_id_type=MESH)
    pl.semaphore_wait(barrier, len(peers))

    started = []

    def send(src, dst, peer):
        i = len(started)
        copy = pltpu.make_async_remote_copy(
            src_ref=src, dst_ref=dst, send_sem=send_sem.at[i], recv_sem=recv_sem.at[i],
            device_id=peer, device_id_type=MESH,
        )
        copy.start()
        started.append(copy)
        return copy

    def gather_row(k):
        def whole(owner):
            return xg[k].at[owner]

        def part(owner, h):
            return xg[k].at[owner, pl.ds(16 * h, 16)]

        rz = at_z[0]
        to_z = send(xt.at[k], whole(r), at_z)
        up = send(xt.at[k], whole(r), at_y(1))
        down = send(xt.at[k], whole(r), at_y(3))
        inside = [send(xt.at[k], whole(r), at_core)]
        xg[k][r] = xt[k]
        yield
        to_z.wait_recv()
        up_z = send(whole(rz), whole(rz), at_y(1))
        down_z = send(whole(rz), whole(rz), at_y(3))
        inside.append(send(whole(rz), whole(rz), at_core))
        yield
        relays = []
        for copy, by, base in ((up, 3, r), (down, 1, r), (up_z, 3, rz), (down_z, 1, rz)):
            owner = turn(y, by) * 4 + base % 4
            copy.wait_recv()
            if by == 3:
                relays.append(send(part(owner, 0), part(owner, 0), at_y(1)))
            else:
                relays.append(send(part(owner, 1), part(owner, 1), at_y(3)))
            inside.append(send(whole(owner), whole(owner), at_core))
        yield
        for base, pair in ((r, relays[:2]), (rz, relays[2:])):
            owner = turn(y, 2) * 4 + base % 4
            for copy in pair:
                copy.wait_recv()
            inside.append(send(whole(owner), whole(owner), at_core))
        yield
        for copy in inside:
            copy.wait_recv()
        yield

    def sweep(load, dims, base):
        def step(u, total):
            for v in range(UNROLL):
                t = u * UNROLL + v
                block = tiles[table[base, t]]
                product = dot(load(table[base + 1, t]), block, dims)
                total = jnp.where(table[base + 2, t] > 0, product, total + product)
                run[t] = total
            return total

        lax.fori_loop(0, SLOTS // UNROLL, step, jnp.zeros((CHUNK, TILE), F32))

    def segment(base, d):
        return jnp.where(table[base + 4, d] > 0, run[table[base + 3, d]], 0.0)

    def loop(n, f):
        def step(i, carry):
            f(i)
            return carry

        lax.fori_loop(0, n, step, 0)

    def reduce_col(k):
        sweep(lambda s: xg[k][:, s].reshape(CHUNK, TILE), NT, 0)
        far, nxt, prv, own = (8 * turn(x, by) for by in (2, 1, 3, 0))

        def rounded(base):
            def one(i):
                ys[k, base + i] = segment(0, base + i).astype(BF16)

            loop(8, one)

        rounded(far)
        relay_l = send(ys.at[k, pl.ds(far, 4)], xrl.at[k], at_x(1))
        relay_r = send(ys.at[k, pl.ds(far + 4, 4)], xrr.at[k], at_x(3))
        rounded(nxt)
        plain_l = send(ys.at[k, pl.ds(nxt + 4, 4)], xinl.at[k, pl.ds(4, 4)], at_x(1))
        rounded(prv)
        plain_r = send(ys.at[k, pl.ds(prv, 4)], xinr.at[k, pl.ds(0, 4)], at_x(3))

        def kept(i):
            yown[k, i] = segment(0, own + i)

        loop(8, kept)
        yield

        def passed_l(i):
            ys[k, nxt + i] = (ys[k, nxt + i].astype(F32) + xrl[k, i].astype(F32)).astype(BF16)

        def passed_r(i):
            ys[k, prv + 4 + i] = (ys[k, prv + 4 + i].astype(F32) + xrr[k, i].astype(F32)).astype(BF16)

        relay_l.wait_recv()
        loop(4, passed_l)
        sum_l = send(ys.at[k, pl.ds(nxt, 4)], xinl.at[k, pl.ds(0, 4)], at_x(1))
        relay_r.wait_recv()
        loop(4, passed_r)
        sum_r = send(ys.at[k, pl.ds(prv + 4, 4)], xinr.at[k, pl.ds(4, 4)], at_x(3))
        yield
        for copy in (plain_l, plain_r, sum_l, sum_r):
            copy.wait_recv()

        def summed(i):
            total = yown[k, i] + xinl[k, i].astype(F32) + xinr[k, i].astype(F32)
            yown[k, i] = total
            zs[k, i] = total.astype(BF16)

        loop(8, summed)
        far, nxt, prv, own = (2 * turn(zh, by) for by in (2, 1, 3, 0))
        relay_l = send(zs.at[k, far], zrl.at[k], at_h(1))
        relay_r = send(zs.at[k, far + 1], zrr.at[k], at_h(3))
        plain_l = send(zs.at[k, nxt + 1], zinl.at[k, 1], at_h(1))
        plain_r = send(zs.at[k, prv], zinr.at[k, 0], at_h(3))
        yield
        relay_l.wait_recv()
        zs[k, nxt] = (yown[k, nxt] + zrl[k].astype(F32)).astype(BF16)
        sum_l = send(zs.at[k, nxt], zinl.at[k, 0], at_h(1))
        relay_r.wait_recv()
        zs[k, prv + 1] = (yown[k, prv + 1] + zrr[k].astype(F32)).astype(BF16)
        sum_r = send(zs.at[k, prv + 1], zinr.at[k, 1], at_h(3))
        yield
        for copy in (plain_l, plain_r, sum_l, sum_r):
            copy.wait_recv()
        for i in range(2):
            total = yown[k, own + i] + zinl[k, i].astype(F32) + zinr[k, i].astype(F32)
            aggt[k, :, i * TILE : (i + 1) * TILE] = total.astype(BF16)
        yield

    def gather_col(k):
        def whole(by_x, by_h):
            return gg[k].at[pl.ds(2 * (turn(x, by_x) * 4 + turn(zh, by_h)), 2)]

        def half(by_h, i):
            return gg[k].at[2 * (x * 4 + turn(zh, by_h)) + i]

        right, left = {}, {}

        def along_x(by_h):
            right[by_h] = send(whole(0, by_h), whole(0, by_h), at_x(1))
            left[by_h] = send(whole(0, by_h), whole(0, by_h), at_x(3))

        up = send(whole(0, 0), whole(0, 0), at_h(1))
        down = send(whole(0, 0), whole(0, 0), at_h(3))
        yield
        along_x(0)
        yield
        up.wait_recv()
        relay_up = send(half(3, 0), half(3, 0), at_h(1))
        along_x(3)
        down.wait_recv()
        relay_down = send(half(1, 1), half(1, 1), at_h(3))
        along_x(1)
        yield
        relay_up.wait_recv()
        relay_down.wait_recv()
        along_x(2)
        yield
        relays = []
        for by_h in (0, 3, 1, 2):
            right[by_h].wait_recv()
            if by_h in (0, 1):
                relays.append(send(whole(3, by_h), whole(3, by_h), at_x(1)))
            left[by_h].wait_recv()
            if by_h in (2, 3):
                relays.append(send(whole(1, by_h), whole(1, by_h), at_x(3)))
        yield
        for copy in relays:
            copy.wait_recv()
        yield

    def reduce_row(k):
        sweep(lambda d: gg[k][d], NN, 5)

        def split(s):
            both = segment(5, s).reshape(8, 2, 16, TILE)
            bown[k, :, s] = jnp.where(core == 0, both[:, 0], both[:, 1])
            bsend[k, :, s] = jnp.where(core == 0, both[:, 1], both[:, 0]).astype(BF16)

        loop(TILES, split)
        far, nxt, prv, own = (2 * turn(y, by) for by in (2, 1, 3, 0))
        inside = [send(bsend.at[k, pl.ds(b, 2)], cin.at[k, pl.ds(b, 2)], at_core) for b in (far, nxt, prv, own)]
        yield

        def joined(base):
            for i in range(2):
                def rows(h):
                    cut = pl.ds(h * 8, 8)
                    total = bown[k, base + i, cut] + cin[k, base + i, cut].astype(F32)
                    bown[k, base + i, cut] = total
                    yb[k, base + i, cut] = total.astype(BF16)

                loop(4, rows)

        inside[0].wait_recv()
        joined(far)
        relay_l = send(yb.at[k, far], yrl.at[k], at_y(1))
        relay_r = send(yb.at[k, far + 1], yrr.at[k], at_y(3))
        inside[1].wait_recv()
        joined(nxt)
        plain_l = send(yb.at[k, nxt + 1], yinl.at[k, 1], at_y(1))
        inside[2].wait_recv()
        joined(prv)
        plain_r = send(yb.at[k, prv], yinr.at[k, 0], at_y(3))
        inside[3].wait_recv()
        joined(own)
        yield

        def passed(at, came):
            def rows(h):
                cut = pl.ds(h * 8, 8)
                yb[k, at, cut] = (bown[k, at, cut] + came[k, cut].astype(F32)).astype(BF16)

            loop(4, rows)

        relay_l.wait_recv()
        passed(nxt, yrl)
        sum_l = send(yb.at[k, nxt], yinl.at[k, 0], at_y(1))
        relay_r.wait_recv()
        passed(prv + 1, yrr)
        sum_r = send(yb.at[k, prv + 1], yinr.at[k, 1], at_y(3))
        yield
        for copy in (plain_l, plain_r, sum_l, sum_r):
            copy.wait_recv()

        def total_of(i, cut):
            return bown[k, own + i, cut] + yinl[k, i, cut].astype(F32) + yinr[k, i, cut].astype(F32)

        def leaving(h):
            cut = pl.ds(h * 8, 8)
            zout[k, cut] = total_of(1 - zl, cut).astype(BF16)

        loop(4, leaving)
        to_z = send(zout.at[k], zpin.at[k], at_z)
        yield
        to_z.wait_recv()

        def final(h):
            cut = pl.ds(h * 8, 8)
            gft[k, cut] = (total_of(zl, cut) + zpin[k, cut].astype(F32)).astype(BF16)

        loop(4, final)
        yield

    def reduce_weight():
        rows_z = pl.multiple_of(128 * zl, 128)
        rows_y = pl.multiple_of(rows_z + 32 * y, 32)
        rows_x = pl.multiple_of(rows_y + 8 * x, 8)
        lanes = pl.multiple_of(128 * zh, 128)
        copy = send(gsum.at[1 - core], rin_c, at_core)
        yield
        copy.wait_recv()
        gsum[core] += rin_c[...]
        copy = send(gsum.at[core, pl.ds(pl.multiple_of(128 - rows_z, 128), 128)], rin_z, at_z)
        yield
        copy.wait_recv()
        gsum[core, pl.ds(rows_z, 128)] += rin_z[...]
        copies = [
            send(
                gsum.at[core, pl.ds(pl.multiple_of(rows_z + 32 * turn(y, by), 32), 32)],
                rin_y.at[by - 1], at_y(by),
            )
            for by in (1, 2, 3)
        ]
        yield
        for copy in copies:
            copy.wait_recv()
        gsum[core, pl.ds(rows_y, 32)] += rin_y[0] + rin_y[1] + rin_y[2]
        copies = [
            send(
                gsum.at[core, pl.ds(pl.multiple_of(rows_y + 8 * turn(x, by), 8), 8)],
                rin_x.at[by - 1], at_x(by),
            )
            for by in (1, 2, 3)
        ]
        yield
        for copy in copies:
            copy.wait_recv()
        gsum[core, pl.ds(rows_x, 8)] += rin_x[0] + rin_x[1] + rin_x[2]
        copies = [
            send(
                gsum.at[core, pl.ds(rows_x, 8), pl.ds(pl.multiple_of(128 * turn(zh, by), 128), 128)],
                rin_h.at[by - 1], at_h(by),
            )
            for by in (1, 2, 3)
        ]
        yield
        for copy in copies:
            copy.wait_recv()
        corner = (core, pl.ds(rows_x, 8), pl.ds(lanes, 128))
        gout[corner] = gsum[corner] + rin_h[0] + rin_h[1] + rin_h[2]
        for cut, where in (
            (corner, [at_h(by) for by in (1, 2, 3)]),
            ((core, pl.ds(rows_x, 8)), [at_x(by) for by in (1, 2, 3)]),
            ((core, pl.ds(rows_y, 32)), [at_y(by) for by in (1, 2, 3)]),
            ((core, pl.ds(rows_z, 128)), [at_z]),
            ((core,), [at_core]),
        ):
            copies = [send(gout.at[cut], gout.at[cut], peer) for peer in where]
            yield
            for copy in copies:
                copy.wait_recv()
        for k in range(2):
            gw[:, k] = gout[k].reshape(16, 16, WIDTH)
        yield

    rows = [gather_row(k) for k in range(2)]
    cols = [reduce_col(k) for k in range(2)]
    for _ in range(3):
        next(rows[0])
    next(rows[1])
    next(rows[0])
    next(rows[0])
    next(cols[0])
    for _ in range(2):
        next(rows[1])
    next(cols[0])
    for _ in range(2):
        next(rows[1])
    next(cols[1])
    next(cols[0])
    next(cols[1])
    next(cols[0])
    next(cols[0])
    for _ in range(3):
        next(cols[1])

    for n in range(2):
        cut = slice(n * CHUNK, (n + 1) * CHUNK)
        pre = jnp.zeros((CHUNK, CHUNK), F32)
        for k in range(2):
            pre += dot(aggt[k], weight[:, k, :, cut].reshape(CHUNK, CHUNK), TN)
        low = jnp.exp(jnp.minimum(pre, 0.0))
        hid[:, cut] = jnp.where(pre > 0, pre, low - 1.0).astype(BF16)
        slope = jnp.where(pre > 0, 1.0, low)
        gpre[:, cut] = (cot[:, cut].astype(F32) * slope).astype(BF16)

    def grad_agg(k):
        made = dot(weight[:, k].reshape(CHUNK, WIDTH), gpre[...], NT).astype(BF16)
        for i in range(2):
            gg[k][2 * c + i] = made[:, i * TILE : (i + 1) * TILE]

    cols = [gather_col(k) for k in range(2)]
    rows = [reduce_row(k) for k in range(2)]
    total = reduce_weight()
    grad_agg(0)
    next(cols[0])
    next(cols[0])
    grad_agg(1)
    next(cols[1])
    for k in range(2):
        gsum[k] = dot(aggt[k], gpre[...], NN)
    next(total)
    next(cols[0])
    next(cols[0])
    next(total)
    next(cols[0])
    next(cols[1])
    next(cols[1])
    next(cols[1])
    next(total)
    next(cols[0])
    next(rows[0])
    next(total)
    next(cols[1])
    next(rows[0])
    next(total)
    next(rows[0])
    next(total)
    next(cols[1])
    next(rows[1])
    next(total)
    next(rows[0])
    next(rows[1])
    next(total)
    next(rows[0])
    next(rows[1])
    next(total)
    next(rows[1])
    next(total)
    next(rows[1])
    next(total)
    for copy in started:
        copy.wait_send()


def body(node_features, layer_weight, tile_values, tile_coords, tile_count, cotangent):
    coords = tile_coords[0, 0]
    live = jnp.arange(SLOTS) < tile_count[0, 0]
    table = jnp.concatenate(
        [order_table(coords[:, 0], coords[:, 1], live), order_table(coords[:, 1], coords[:, 0], live)]
    )
    xt = node_features.reshape(TILES, TILE, 2, 16).transpose(2, 0, 3, 1)
    vmem = pl.BlockSpec(memory_space=pltpu.VMEM)
    slab = (CHUNK, TILE)
    bits = (TILES, 16, TILE)
    hid, gw, gft = pl.pallas_call(
        kernel,
        out_shape=[
            jax.ShapeDtypeStruct((CHUNK, WIDTH), BF16),
            jax.ShapeDtypeStruct((16, 2, 16, WIDTH), F32),
            jax.ShapeDtypeStruct((2,) + bits, BF16),
        ],
        in_specs=[pl.BlockSpec(memory_space=pltpu.SMEM)] + [vmem] * 4,
        out_specs=[vmem] * 3,
        scratch_shapes=[
            pltpu.VMEM((16,) + bits, BF16),
            pltpu.VMEM((16,) + bits, BF16),
            pltpu.VMEM((SLOTS,) + slab, F32),
            pltpu.VMEM((2, TILES) + slab, BF16),
            pltpu.VMEM((2, 8) + slab, F32),
            pltpu.VMEM((2, 4) + slab, BF16),
            pltpu.VMEM((2, 4) + slab, BF16),
            pltpu.VMEM((2, 8) + slab, BF16),
            pltpu.VMEM((2, 8) + slab, BF16),
            pltpu.VMEM((2, 8) + slab, BF16),
            pltpu.VMEM((2,) + slab, BF16),
            pltpu.VMEM((2,) + slab, BF16),
            pltpu.VMEM((2, 2) + slab, BF16),
            pltpu.VMEM((2, 2) + slab, BF16),
            pltpu.VMEM((2, CHUNK, CHUNK), BF16),
            pltpu.VMEM((CHUNK, WIDTH), BF16),
            pltpu.VMEM((TILES,) + slab, BF16),
            pltpu.VMEM((TILES,) + slab, BF16),
            pltpu.VMEM((2, 8) + bits, F32),
            pltpu.VMEM((2, 8) + bits, BF16),
            pltpu.VMEM((2, 8) + bits, BF16),
            pltpu.VMEM((2, 8) + bits, BF16),
            pltpu.VMEM((2,) + bits, BF16),
            pltpu.VMEM((2,) + bits, BF16),
            pltpu.VMEM((2, 2) + bits, BF16),
            pltpu.VMEM((2, 2) + bits, BF16),
            pltpu.VMEM((2,) + bits, BF16),
            pltpu.VMEM((2,) + bits, BF16),
            pltpu.VMEM((2, CHUNK, WIDTH), F32),
            pltpu.VMEM((2, CHUNK, WIDTH), F32),
            pltpu.VMEM((CHUNK, WIDTH), F32),
            pltpu.VMEM((128, WIDTH), F32),
            pltpu.VMEM((3, 32, WIDTH), F32),
            pltpu.VMEM((3, 8, WIDTH), F32),
            pltpu.VMEM((3, 8, 128), F32),
            pltpu.SemaphoreType.DMA((WIRES,)),
            pltpu.SemaphoreType.DMA((WIRES,)),
        ],
        compiler_params=pltpu.CompilerParams(
            collective_id=0, has_side_effects=True, vmem_limit_bytes=62 * 1024 * 1024
        ),
    )(
        table,
        xt,
        tile_values.reshape(SLOTS, TILE, TILE),
        layer_weight.reshape(16, 2, 16, WIDTH),
        cotangent,
    )
    grad_features = gft.transpose(1, 3, 0, 2).reshape(TILES * TILE, 32)
    return hid, gw.reshape(WIDTH, WIDTH), grad_features


def solution(mesh):
    in_specs = (
        P("col", "row"),
        P(),
        P("row", "col", None, None, None),
        P("row", "col", None, None),
        P("row", "col"),
        P(("row", "col"), None),
    )
    out_specs = (P(("row", "col"), None), P(), P("col", "row"))
    return jax.shard_map(body, mesh=mesh, in_specs=in_specs, out_specs=out_specs, check_vma=False)
```

time: 842 us -> 171 us (0.20)
  waiting for transfers between devices: 592 us -> 0 us
  Pallas kernels: 0 us -> 156 us
  other arithmetic: 117 us -> 3.17 us
  local copies, waits for them, and re-layouts: 67.4 us -> 8.78 us
  matrix products: 49 us -> 0 us
  between operations: 14.4 us -> 1.35 us
    psum x1 -> x0, waiting for transfers between devices: 258 us -> none  [body(): grad_weight = lax.psum(weight_term, ('row', 'col'))]
    reduce_scatter x2 -> x0, waiting for transfers between devices: 219 us -> none  [the longest x1 121 us: body(): lax.psum_scatter(partial_value, 'col', scatter_dimension=0, tiled=True)]
    pallas_call x0 -> x1, Pallas kernels: none -> 156 us  [body(): pl.pallas_call(kernel, out_shape=[jax.ShapeDtypeStruct((CHUNK, WIDTH), BF...]
    scatter-add x12 -> x0, other arithmetic: 115 us -> none  [one_turn(): return (totals.at[placed].add(product), None)]
    all_gather x2 -> x0, waiting for transfers between devices: 113 us -> none  [the longest x1 70 us: body(): block_grads = lax.all_gather(grad_agg, 'col', axis=0, tiled=True)]
    dot_general x15 -> x0, matrix products: 49 us -> none  [the longest x6 22.3 us: one_turn(): jnp.einsum('tab,tak->tbk', block_tiles, gathered_rows, preferred_element_...]
    gather x12 -> x0, local copies, waits for them, and re-layouts: 34.4 us -> none  [one_turn(): gathered_rows = source_tiles[picked]]
    another operation x4 -> x0, local copies, waits for them, and re-layouts: 8.74 us -> none
  transfers between devices with their start and end apart: 5 -> 0, of which waited for: 5 -> 0; matrix products, arithmetic and copies ran while one was open for 1% -> 0% of each run, Pallas kernels for 0% -> 0%
where the time goes in v1:
time: 171 us; the launch traced here: 169 us
  Pallas kernels  156 us (91%)
  local copies, waits for them, and re-layouts  8.78 us (5%)
  other arithmetic  3.17 us (2%)
    pallas_call x1, Pallas kernels, body(): pl.pallas_call(kernel, out_shape=[jax.ShapeDtypeStruct((CHUNK, WIDTH), BF...  156 us
    unnamed x4, local copies, waits for them, and re-layouts  5.73 us

profile of v1, /device:TPU:2, one launch (start us, length us, event | category | flops | bytes accessed | tf_op | source)
XLA Modules:
  0.0 169.5 jit_solution(9681414562282559827)
XLA Ops:
  1.3 0.8 fusion.16
  2.1 0.8 compare_select_fusion
  2.8 0.8 fusion.12
  3.6 0.2 fusion.8
  3.8 0.2 fusion
  4.0 0.1 convert_reduce_fusion
  4.2 0.1 select_reduce_fusion.1
  4.4 0.1 select_reduce_fusion
  4.5 1.2 concatenate.3.table
  5.7 1.0 copy.13
  6.7 0.8 copy.18
  7.5 156.2 %shard_map.85 = (bf16[256,512]{1,0:T(8,128)(2,1)}, f32[16,2,16,512]{3,2,1,0:T(8,128)}, bf16[2,32,16,128]{3,2,1,0:T(8,128)(2,1)}) custom-call(s32[10,96]{1,0:T(8,128)} %concatenate.3.table, bf16[2,32,16,128]{3,2,1,0:T(8,128)(2,1)} %bitcast.52, bf16[96,128,128]{2,1,0:T(8,128)(2,1)} %bitcast.51, bf16[16,2,16,512]{3,2,1,0:T(8,128)(2,1)} %bitcast.56, ...), custom_call_target="tpu_custom_call" | custom-call | tf_op jit(solution)/shard_map/pallas_call | solution.py:484
  163.7 1.0 copy.12
  164.7 0.8 copy.17
  165.5 1.7 copy.22
  167.2 2.3 %copy.23 = f32[512,512]{1,0:T(8,128)} copy(f32[512,512]{1,0:T(8,128)} %bitcast.53) | data formatting | bytes 2097152
  (7 shorter events, 0.1 us)

commit v2 on v1

v2 whole, which is shorter than its diff:
```python
import jax
import jax.numpy as jnp
from jax import lax
from jax.experimental import pallas as pl
from jax.experimental.pallas import tpu as pltpu
from jax.sharding import PartitionSpec as P

MESH = pl.DeviceIdType.MESH
BF16 = jnp.bfloat16
F32 = jnp.float32

SLOTS = 96
TILES = 32
TILE = 128
WIDTH = 512
CHUNK = 128
NODES = 256
UNROLL = 8
WIRES = 192

NT = (((1,), (1,)), ((), ()))
NN = (((1,), (0,)), ((), ()))
TN = (((0,), (0,)), ((), ()))


def dot(a, b, dims):
    return lax.dot_general(a, b, dims, preferred_element_type=F32)


def order_table(main, other, live):
    side = (TILE, TILE)
    lane = lax.broadcasted_iota(jnp.int32, (1, TILE), 1)
    lanes = lax.broadcasted_iota(jnp.int32, side, 1)
    key = jnp.where(live, main * 64 + other, 4096 + lane)
    across = jnp.broadcast_to(key, side)
    down = across.T
    before = down < across
    rank = jnp.sum(before.astype(jnp.int32), axis=0, keepdims=True)
    same = jnp.where(before & ((down >> 6) == (across >> 6)), 1, 0)
    opens = jnp.where(jnp.sum(same, axis=0, keepdims=True) > 0, 0, 1)
    fact = lane + 128 * jnp.where(live, other, 0) + 4096 * opens
    places = jnp.broadcast_to(rank, side).T == lanes
    facts = jnp.sum(jnp.where(places, jnp.broadcast_to(fact, side).T, 0), axis=0, keepdims=True)
    upto = jnp.sum(((down >> 6) <= lanes).astype(jnp.int32), axis=0, keepdims=True)
    count = jnp.sum(((down >> 6) == lanes).astype(jnp.int32), axis=0, keepdims=True)
    return [facts & 127, (facts >> 7) & 31, facts >> 12, jnp.maximum(upto - 1, 0), count]


def kernel(
    count, coords, xin, tiles_hbm, weight_hbm, cot_hbm, hid, gw, gft,
    xg0, xg1, xg2, xg3, run, ys, yown, xrl, xrr, xinl, xinr, zs, zrl, zrr, zinl, zinr,
    aggt, gpre, gg0, gg1, gg2, gg3, bown, bsend, cin, yb, yrl, yrr, yinl, yinr, zout, zpin,
    gsum, gout, rin_c, rin_z, rin_y, rin_x, rin_h, tiles, weight, cot, drawn, made, table,
    send_sem, recv_sem, local_sem,
):
    xg, gg = (xg0, xg1, xg2, xg3), (gg0, gg1, gg2, gg3)
    r = lax.axis_index("row")
    c = lax.axis_index("col")
    y, zl, core = r // 4, (r // 2) % 2, r % 2
    x, zh = c // 4, c % 4

    def turn(v, by):
        return (v + by) % 4

    def at_y(by):
        return (turn(y, by) * 4 + r % 4, c)

    def at_x(by):
        return (r, turn(x, by) * 4 + zh)

    def at_h(by):
        return (r, x * 4 + turn(zh, by))

    at_z = (r + 2 - 4 * zl, c)
    at_core = (r + 1 - 2 * core, c)

    barrier = pltpu.get_barrier_semaphore()
    peers = [at_z, at_core] + [f(by) for f in (at_y, at_x, at_h) for by in (1, 2, 3)]
    for peer in peers:
        pl.semaphore_signal(barrier, inc=1, device_id=peer, device_id_type=MESH)
    moves = [
        pltpu.make_async_copy(src, dst, local_sem.at[i])
        for i, (src, dst) in enumerate(((tiles_hbm, tiles), (weight_hbm, weight), (cot_hbm, cot)))
    ]
    for move in moves:
        move.start()

    def loop(n, f):
        def step(i, carry):
            f(i)
            return carry

        lax.fori_loop(0, n, step, 0)

    place = 2 * y + zl
    place_z = 2 * y + 1 - zl

    def laid_out(s):
        cut = pl.ds(pl.multiple_of(s * TILE, TILE), TILE)
        for k in range(2):
            xg[2 * k][place, s] = xin[16 * k : 16 * k + 16, cut]

    loop(TILES, laid_out)
    pl.semaphore_wait(barrier, len(peers))

    started = []

    def send(src, dst, peer):
        i = len(started)
        copy = pltpu.make_async_remote_copy(
            src_ref=src, dst_ref=dst, send_sem=send_sem.at[i], recv_sem=recv_sem.at[i],
            device_id=peer, device_id_type=MESH,
        )
        copy.start()
        started.append(copy)
        return copy

    def gather_row(k):
        own, across = xg[2 * k], xg[2 * k + 1]

        def part(owner, h):
            return own.at[owner, pl.ds(16 * h, 16)]

        inside = []

        def pass_on(owner):
            inside.append(send(own.at[owner], across.at[owner], at_core))

        to_z = send(own.at[place], own.at[place], at_z)
        up = send(own.at[place], own.at[place], at_y(1))
        down = send(own.at[place], own.at[place], at_y(3))
        pass_on(place)
        yield
        to_z.wait_recv()
        up_z = send(own.at[place_z], own.at[place_z], at_y(1))
        down_z = send(own.at[place_z], own.at[place_z], at_y(3))
        pass_on(place_z)
        yield
        relays = []
        for copy, by, side in ((up, 3, zl), (down, 1, zl), (up_z, 3, 1 - zl), (down_z, 1, 1 - zl)):
            owner = 2 * turn(y, by) + side
            copy.wait_recv()
            if by == 3:
                relays.append(send(part(owner, 0), part(owner, 0), at_y(1)))
            else:
                relays.append(send(part(owner, 1), part(owner, 1), at_y(3)))
            pass_on(owner)
        yield
        for side, pair in ((zl, relays[:2]), (1 - zl, relays[2:])):
            for copy in pair:
                copy.wait_recv()
            pass_on(2 * turn(y, 2) + side)
        yield
        for copy in inside:
            copy.wait_recv()
        yield

    def sweep(load, dims, base):
        def step(u, total):
            for v in range(UNROLL):
                t = u * UNROLL + v
                block = tiles[table[base, t]]
                product = dot(load(table[base + 1, t]), block, dims)
                total = jnp.where(table[base + 2, t] > 0, product, total + product)
                run[t] = total
            return total

        lax.fori_loop(0, SLOTS // UNROLL, step, jnp.zeros((CHUNK, TILE), F32))

    def segment(base, d):
        return jnp.where(table[base + 4, d] > 0, run[table[base + 3, d]], 0.0)

    def reduce_col(k):
        sweep(lambda s: xg[k][:, s].reshape(CHUNK, TILE), NT, 0)
        yield
        far, nxt, prv, own = (8 * turn(x, by) for by in (2, 1, 3, 0))

        def rounded(base):
            def one(i):
                ys[k, base + i] = segment(0, base + i).astype(BF16)

            loop(8, one)

        rounded(far)
        relay_l = send(ys.at[k, pl.ds(far, 4)], xrl.at[k], at_x(1))
        relay_r = send(ys.at[k, pl.ds(far + 4, 4)], xrr.at[k], at_x(3))
        rounded(nxt)
        plain_l = send(ys.at[k, pl.ds(nxt + 4, 4)], xinl.at[k, pl.ds(4, 4)], at_x(1))
        rounded(prv)
        plain_r = send(ys.at[k, pl.ds(prv, 4)], xinr.at[k, pl.ds(0, 4)], at_x(3))

        def kept(i):
            yown[k, i] = segment(0, own + i)

        loop(8, kept)
        yield

        def passed_l(i):
            ys[k, nxt + i] = (ys[k, nxt + i].astype(F32) + xrl[k, i].astype(F32)).astype(BF16)

        def passed_r(i):
            ys[k, prv + 4 + i] = (ys[k, prv + 4 + i].astype(F32) + xrr[k, i].astype(F32)).astype(BF16)

        relay_l.wait_recv()
        loop(4, passed_l)
        sum_l = send(ys.at[k, pl.ds(nxt, 4)], xinl.at[k, pl.ds(0, 4)], at_x(1))
        relay_r.wait_recv()
        loop(4, passed_r)
        sum_r = send(ys.at[k, pl.ds(prv + 4, 4)], xinr.at[k, pl.ds(4, 4)], at_x(3))
        yield
        for copy in (plain_l, plain_r, sum_l, sum_r):
            copy.wait_recv()

        def summed(i):
            total = yown[k, i] + xinl[k, i].astype(F32) + xinr[k, i].astype(F32)
            yown[k, i] = total
            zs[k, i] = total.astype(BF16)

        loop(8, summed)
        far, nxt, prv, own = (2 * turn(zh, by) for by in (2, 1, 3, 0))
        relay_l = send(zs.at[k, far], zrl.at[k], at_h(1))
        relay_r = send(zs.at[k, far + 1], zrr.at[k], at_h(3))
        plain_l = send(zs.at[k, nxt + 1], zinl.at[k, 1], at_h(1))
        plain_r = send(zs.at[k, prv], zinr.at[k, 0], at_h(3))
        yield
        relay_l.wait_recv()
        zs[k, nxt] = (yown[k, nxt] + zrl[k].astype(F32)).astype(BF16)
        sum_l = send(zs.at[k, nxt], zinl.at[k, 0], at_h(1))
        relay_r.wait_recv()
        zs[k, prv + 1] = (yown[k, prv + 1] + zrr[k].astype(F32)).astype(BF16)
        sum_r = send(zs.at[k, prv + 1], zinr.at[k, 1], at_h(3))
        yield
        for copy in (plain_l, plain_r, sum_l, sum_r):
            copy.wait_recv()
        for i in range(2):
            total = yown[k, own + i] + zinl[k, i].astype(F32) + zinr[k, i].astype(F32)
            aggt[k, :, i * TILE : (i + 1) * TILE] = total.astype(BF16)
        yield

    def gather_col(k):
        def whole(by_x, by_h):
            return gg[k].at[pl.ds(2 * (turn(x, by_x) * 4 + turn(zh, by_h)), 2)]

        def half(by_h, i):
            return gg[k].at[2 * (x * 4 + turn(zh, by_h)) + i]

        right, left = {}, {}

        def along_x(by_h):
            right[by_h] = send(whole(0, by_h), whole(0, by_h), at_x(1))
            left[by_h] = send(whole(0, by_h), whole(0, by_h), at_x(3))

        up = send(whole(0, 0), whole(0, 0), at_h(1))
        down = send(whole(0, 0), whole(0, 0), at_h(3))
        yield
        along_x(0)
        yield
        up.wait_recv()
        relay_up = send(half(3, 0), half(3, 0), at_h(1))
        along_x(3)
        down.wait_recv()
        relay_down = send(half(1, 1), half(1, 1), at_h(3))
        along_x(1)
        yield
        relay_up.wait_recv()
        relay_down.wait_recv()
        along_x(2)
        yield
        relays = []
        for by_h in (0, 3, 1, 2):
            right[by_h].wait_recv()
            if by_h in (0, 1):
                relays.append(send(whole(3, by_h), whole(3, by_h), at_x(1)))
            left[by_h].wait_recv()
            if by_h in (2, 3):
                relays.append(send(whole(1, by_h), whole(1, by_h), at_x(3)))
        yield
        for copy in relays:
            copy.wait_recv()
        yield

    def reduce_row(k):
        sweep(lambda d: gg[2 * k + 1][d], NN, 5)

        def leaving_core(s):
            bsend[k, :, s] = segment(5, s).reshape(8, 16, TILE).astype(BF16)

        loop(TILES, leaving_core)
        far, nxt, prv, own = (2 * turn(y, by) for by in (2, 1, 3, 0))
        inside = [send(bsend.at[k, pl.ds(b, 2)], cin.at[k, pl.ds(b, 2)], at_core) for b in (far, nxt, prv, own)]
        yield
        sweep(lambda d: gg[2 * k][d], NN, 5)

        def staying(s):
            bown[k, :, s] = segment(5, s).reshape(8, 16, TILE)

        loop(TILES, staying)

        def joined(base):
            for i in range(2):
                def rows(h):
                    cut = pl.ds(h * 8, 8)
                    total = bown[k, base + i, cut] + cin[k, base + i, cut].astype(F32)
                    bown[k, base + i, cut] = total
                    yb[k, base + i, cut] = total.astype(BF16)

                loop(4, rows)

        inside[0].wait_recv()
        joined(far)
        relay_l = send(yb.at[k, far], yrl.at[k], at_y(1))
        relay_r = send(yb.at[k, far + 1], yrr.at[k], at_y(3))
        inside[1].wait_recv()
        joined(nxt)
        plain_l = send(yb.at[k, nxt + 1], yinl.at[k, 1], at_y(1))
        inside[2].wait_recv()
        joined(prv)
        plain_r = send(yb.at[k, prv], yinr.at[k, 0], at_y(3))
        inside[3].wait_recv()
        joined(own)
        yield

        def passed(at, came):
            def rows(h):
                cut = pl.ds(h * 8, 8)
                yb[k, at, cut] = (bown[k, at, cut] + came[k, cut].astype(F32)).astype(BF16)

            loop(4, rows)

        relay_l.wait_recv()
        passed(nxt, yrl)
        sum_l = send(yb.at[k, nxt], yinl.at[k, 0], at_y(1))
        relay_r.wait_recv()
        passed(prv + 1, yrr)
        sum_r = send(yb.at[k, prv + 1], yinr.at[k, 1], at_y(3))
        yield
        for copy in (plain_l, plain_r, sum_l, sum_r):
            copy.wait_recv()

        def total_of(i, cut):
            return bown[k, own + i, cut] + yinl[k, i, cut].astype(F32) + yinr[k, i, cut].astype(F32)

        def leaving(h):
            cut = pl.ds(h * 8, 8)
            zout[k, cut] = total_of(1 - zl, cut).astype(BF16)

        loop(4, leaving)
        to_z = send(zout.at[k], zpin.at[k], at_z)
        yield
        to_z.wait_recv()

        def final(s):
            cut = pl.ds(pl.multiple_of(s * TILE, TILE), TILE)
            gft[16 * k : 16 * k + 16, cut] = (total_of(zl, s) + zpin[k, s].astype(F32)).astype(BF16)

        loop(TILES, final)
        yield

    def reduce_weight():
        rows_y = pl.multiple_of(32 * y, 32)
        rows_x = pl.multiple_of(rows_y + 8 * x, 8)
        lanes = pl.multiple_of(128 * zh, 128)
        copy = send(gsum.at[1 - core], rin_c, at_core)
        yield
        copy.wait_recv()
        gsum[core] += rin_c[...]
        copy = send(gsum.at[core, 1 - zl], rin_z, at_z)
        yield
        copy.wait_recv()
        gsum[core, zl] += rin_z[...]
        copies = [
            send(
                gsum.at[core, zl, pl.ds(pl.multiple_of(32 * turn(y, by), 32), 32)],
                rin_y.at[by - 1], at_y(by),
            )
            for by in (1, 2, 3)
        ]
        yield
        for copy in copies:
            copy.wait_recv()
        gsum[core, zl, pl.ds(rows_y, 32)] += rin_y[0] + rin_y[1] + rin_y[2]
        copies = [
            send(
                gsum.at[core, zl, pl.ds(pl.multiple_of(rows_y + 8 * turn(x, by), 8), 8)],
                rin_x.at[by - 1], at_x(by),
            )
            for by in (1, 2, 3)
        ]
        yield
        for copy in copies:
            copy.wait_recv()
        gsum[core, zl, pl.ds(rows_x, 8)] += rin_x[0] + rin_x[1] + rin_x[2]
        copies = [
            send(
                gsum.at[core, zl, pl.ds(rows_x, 8), pl.ds(pl.multiple_of(128 * turn(zh, by), 128), 128)],
                rin_h.at[by - 1], at_h(by),
            )
            for by in (1, 2, 3)
        ]
        yield
        for copy in copies:
            copy.wait_recv()
        corner = (core, zl, pl.ds(rows_x, 8), pl.ds(lanes, 128))
        gout[corner] = gsum[corner] + rin_h[0] + rin_h[1] + rin_h[2]
        for cut, where in (
            (corner, [at_h(by) for by in (1, 2, 3)]),
            ((core, zl, pl.ds(rows_x, 8)), [at_x(by) for by in (1, 2, 3)]),
            ((core, zl, pl.ds(rows_y, 32)), [at_y(by) for by in (1, 2, 3)]),
            ((core, zl), [at_z]),
            ((core,), [at_core]),
        ):
            copies = [send(gout.at[cut], gout.at[cut], peer) for peer in where]
            yield
            for copy in copies:
                copy.wait_recv()
        for h in range(2):
            for k in range(2):
                gw[:, h, k] = gout[h, k].reshape(8, 16, WIDTH)
        yield

    def go(gen, times=1):
        for _ in range(times):
            next(gen)

    rows = [gather_row(k) for k in range(2)]
    cols = [reduce_col(q) for q in range(4)]
    go(rows[0])
    drawn[...] = jnp.zeros((8, TILE), jnp.int32)
    drawn[0:2, 0:SLOTS] = coords[...]
    dest, source = drawn[0:1, :], drawn[1:2, :]
    live = lax.broadcasted_iota(jnp.int32, (1, TILE), 1) < count[0, 0]
    for i, row in enumerate(order_table(dest, source, live) + order_table(source, dest, live)):
        made[i : i + 1, :] = row
    to_table = pltpu.make_async_copy(made, table, local_sem.at[3])
    to_table.start()
    go(rows[0], 2)
    go(rows[1])
    to_table.wait()
    for move in moves:
        move.wait()
    go(rows[0])
    go(cols[0], 2)
    go(rows[1])
    go(rows[0])
    go(cols[1])
    go(cols[0])
    go(cols[1])
    go(rows[1], 2)
    go(cols[2])
    go(cols[1])
    go(cols[2])
    go(cols[0])
    go(rows[1])
    go(cols[3])
    go(cols[2])
    go(cols[3])
    go(cols[0])
    go(cols[1])
    go(cols[0])
    go(cols[3])
    go(cols[1])
    go(cols[2])
    go(cols[1])
    go(cols[2])
    go(cols[3])
    go(cols[2])
    go(cols[3], 2)

    def core_of(q):
        return core if q % 2 == 0 else 1 - core

    for n in range(2):
        cut = slice(n * NODES, (n + 1) * NODES)
        pre = jnp.zeros((NODES, NODES), F32)
        for q in range(4):
            pre += dot(aggt[q], weight[:, core_of(q), q // 2, :, cut].reshape(CHUNK, NODES), TN)
        low = jnp.exp(jnp.minimum(pre, 0.0))
        hid[:, cut] = jnp.where(pre > 0, pre, low - 1.0).astype(BF16)
        slope = jnp.where(pre > 0, 1.0, low)
        gpre[:, cut] = (cot[:, cut].astype(F32) * slope).astype(BF16)

    def grad_agg(q):
        part = dot(weight[:, core_of(q), q // 2].reshape(CHUNK, WIDTH), gpre[...], NT).astype(BF16)
        for i in range(2):
            gg[q][2 * c + i] = part[:, i * TILE : (i + 1) * TILE]

    a, b, d, e = 1, 0, 3, 2
    cols = [gather_col(q) for q in range(4)]
    rows = [reduce_row(k) for k in range(2)]
    total = reduce_weight()
    grad_agg(a)
    go(cols[a], 2)
    for q in (b, d, e):
        grad_agg(q)
    for q in range(4):
        gsum[core_of(q), q // 2] = dot(aggt[q], gpre[...], NN)
    go(cols[a])
    go(cols[b])
    go(total)
    go(cols[a])
    go(cols[b], 3)
    go(total)
    go(cols[a])
    go(cols[d], 3)
    go(total)
    go(cols[b])
    go(cols[d])
    go(total)
    go(cols[a])
    go(rows[0])
    go(cols[e], 3)
    go(cols[d])
    go(cols[e])
    go(total)
    go(cols[b])
    go(rows[0])
    go(total)
    go(cols[e])
    go(cols[d])
    go(rows[1])
    go(total)
    go(rows[0])
    go(total)
    go(cols[e])
    go(rows[1])
    go(total)
    go(rows[0])
    go(rows[1])
    go(total)
    go(rows[0])
    go(rows[1])
    go(total)
    go(rows[1])
    for copy in started:
        copy.wait_send()


def hand_over(*refs):
    sources, targets, sems = refs[:3], refs[3:6], refs[6]
    copies = [pltpu.make_async_copy(s, t, sems.at[i]) for i, (s, t) in enumerate(zip(sources, targets))]
    for copy in copies:
        copy.start()
    for copy in copies:
        copy.wait()


def body(node_features, layer_weight, tile_values, tile_coords, tile_count, cotangent):
    vmem = pl.BlockSpec(memory_space=pltpu.VMEM)
    smem = pl.BlockSpec(memory_space=pltpu.SMEM)
    hbm = pl.BlockSpec(memory_space=pl.ANY)
    slab = (CHUNK, TILE)
    bits = (TILES, 16, TILE)
    shapes = [
        jax.ShapeDtypeStruct((NODES, WIDTH), BF16),
        jax.ShapeDtypeStruct((8, 2, 2, 16, WIDTH), F32),
        jax.ShapeDtypeStruct((32, TILES * TILE), BF16),
    ]
    results = pl.pallas_call(
        kernel,
        out_shape=shapes,
        in_specs=[smem, vmem, vmem, hbm, hbm, hbm],
        out_specs=[vmem] * 3,
        scratch_shapes=[
            *[pltpu.VMEM((8,) + bits, BF16)] * 4,
            pltpu.VMEM((SLOTS,) + slab, F32),
            pltpu.VMEM((4, TILES) + slab, BF16),
            pltpu.VMEM((4, 8) + slab, F32),
            pltpu.VMEM((4, 4) + slab, BF16),
            pltpu.VMEM((4, 4) + slab, BF16),
            pltpu.VMEM((4, 8) + slab, BF16),
            pltpu.VMEM((4, 8) + slab, BF16),
            pltpu.VMEM((4, 8) + slab, BF16),
            pltpu.VMEM((4,) + slab, BF16),
            pltpu.VMEM((4,) + slab, BF16),
            pltpu.VMEM((4, 2) + slab, BF16),
            pltpu.VMEM((4, 2) + slab, BF16),
            pltpu.VMEM((4, CHUNK, NODES), BF16),
            pltpu.VMEM((NODES, WIDTH), BF16),
            *[pltpu.VMEM((TILES,) + slab, BF16)] * 4,
            pltpu.VMEM((2, 8) + bits, F32),
            pltpu.VMEM((2, 8) + bits, BF16),
            pltpu.VMEM((2, 8) + bits, BF16),
            pltpu.VMEM((2, 8) + bits, BF16),
            pltpu.VMEM((2,) + bits, BF16),
            pltpu.VMEM((2,) + bits, BF16),
            pltpu.VMEM((2, 2) + bits, BF16),
            pltpu.VMEM((2, 2) + bits, BF16),
            pltpu.VMEM((2,) + bits, BF16),
            pltpu.VMEM((2,) + bits, BF16),
            pltpu.VMEM((2, 2, 128, WIDTH), F32),
            pltpu.VMEM((2, 2, 128, WIDTH), F32),
            pltpu.VMEM((2, 128, WIDTH), F32),
            pltpu.VMEM((128, WIDTH), F32),
            pltpu.VMEM((3, 32, WIDTH), F32),
            pltpu.VMEM((3, 8, WIDTH), F32),
            pltpu.VMEM((3, 8, 128), F32),
            pltpu.VMEM((SLOTS, TILE, TILE), BF16),
            pltpu.VMEM((8, 2, 2, 16, WIDTH), BF16),
            pltpu.VMEM((NODES, WIDTH), BF16),
            pltpu.VMEM((8, TILE), jnp.int32),
            pltpu.VMEM((16, TILE), jnp.int32),
            pltpu.SMEM((16, TILE), jnp.int32),
            pltpu.SemaphoreType.DMA((WIRES,)),
            pltpu.SemaphoreType.DMA((WIRES,)),
            pltpu.SemaphoreType.DMA((4,)),
        ],
        compiler_params=pltpu.CompilerParams(
            collective_id=0, has_side_effects=True, vmem_limit_bytes=62 * 1024 * 1024
        ),
    )(
        tile_count,
        tile_coords.reshape(SLOTS, 2).T,
        node_features.T,
        tile_values.reshape(SLOTS, TILE, TILE),
        layer_weight.reshape(8, 2, 2, 16, WIDTH),
        cotangent,
    )
    hid, gw, gft = pl.pallas_call(
        hand_over,
        out_shape=shapes,
        in_specs=[vmem] * 3,
        out_specs=[hbm] * 3,
        scratch_shapes=[pltpu.SemaphoreType.DMA((3,))],
    )(*results)
    return hid, gw.reshape(WIDTH, WIDTH), gft.T


def solution(mesh):
    in_specs = (
        P("col", "row"),
        P(),
        P("row", "col", None, None, None),
        P("row", "col", None, None),
        P("row", "col"),
        P(("row", "col"), None),
    )
    out_specs = (P(("row", "col"), None), P(), P("col", "row"))
    return jax.shard_map(body, mesh=mesh, in_specs=in_specs, out_specs=out_specs, check_vma=False)
```

time: 171 us -> 154 us (0.901)
  local copies, waits for them, and re-layouts: 8.78 us -> 0 us
  Pallas kernels: 156 us -> 150 us
  other arithmetic: 3.17 us -> 0 us
    pallas_call x1 -> x2, Pallas kernels: 156 us -> 150 us  [the longest x1 147 us: body(): pl.pallas_call(kernel, out_shape=shapes, in_specs=[smem, vmem, vmem, hbm,...]
    unnamed x4 -> x0, local copies, waits for them, and re-layouts: 5.73 us -> none
where the time goes in v2:
time: 154 us; the launch traced here: 151 us
  Pallas kernels  150 us (97%)
    pallas_call x1, Pallas kernels, body(): pl.pallas_call(kernel, out_shape=shapes, in_specs=[smem, vmem, vmem, hbm,...  147 us

profile of v2, /device:TPU:2, one launch (start us, length us, event | category | flops | bytes accessed | tf_op | source)
XLA Modules:
  0.0 151.3 jit_solution(11801426480330332226)
XLA Ops:
  1.3 147.5 %shard_map.85 = (bf16[256,512]{1,0:T(8,128)(2,1)}, f32[8,2,2,16,512]{4,3,2,1,0:T(8,128)}, bf16[32,4096]{1,0:T(8,128)(2,1)}) custom-call(s32[1,1]{1,0:T(1,128)S(6)} %copy.9.count, s32[2,96]{1,0:T(2,128)} %bitcast.11, bf16[32,4096]{1,0:T(8,128)(2,1)} %bitcast.10, bf16[96,128,128]{2,1,0:T(8,128)(2,1)} %bitcast.8, bf16[8,2,2,16,512]{4,3,2,1,0:T(8,128)(2,1)} %bitcast.9, ...), custom_call_target="tpu_custom_call" | custom-call | tf_op jit(solution)/shard_map/pallas_call | solution.py:558
  148.8 2.5 %shard_map.86 = (bf16[256,512]{1,0:T(8,128)(2,1)}, f32[8,2,2,16,512]{4,3,2,1,0:T(8,128)}, bf16[32,4096]{1,0:T(8,128)(2,1)}) custom-call(bf16[256,512]{1,0:T(8,128)(2,1)} %get-tuple-element.9.refs_0_, f32[8,2,2,16,512]{4,3,2,1,0:T(8,128)} %get-tuple-element.10.refs_1_, bf16[32,4096]{1,0:T(8,128)(2,1)} %get-tuple-element.11.refs_2_), custom_call_target="tpu_custom_call" | custom-call | tf_op jit(solution)/shard_map/pallas_call | solution.py:618

commit v3 on v2

--- a/solution.py
+++ b/solution.py
@@ -170,27 +170,33 @@
     def segment(base, d):
         return jnp.where(table[base + 4, d] > 0, run[table[base + 3, d]], 0.0)
 
-    def reduce_col(k):
+    def reduce_col(k, z_first):
+        spot_a, spot_b = (zh, x) if z_first else (x, zh)
+        at_a, at_b = (at_h, at_x) if z_first else (at_x, at_h)
+
+        def tile_of(base, i):
+            return (i // 2) * 8 + base // 4 + i % 2 if z_first else base + i
+
         sweep(lambda s: xg[k][:, s].reshape(CHUNK, TILE), NT, 0)
         yield
-        far, nxt, prv, own = (8 * turn(x, by) for by in (2, 1, 3, 0))
+        far, nxt, prv, own = (8 * turn(spot_a, by) for by in (2, 1, 3, 0))
 
         def rounded(base):
             def one(i):
-                ys[k, base + i] = segment(0, base + i).astype(BF16)
+                ys[k, base + i] = segment(0, tile_of(base, i)).astype(BF16)
 
             loop(8, one)
 
         rounded(far)
-        relay_l = send(ys.at[k, pl.ds(far, 4)], xrl.at[k], at_x(1))
-        relay_r = send(ys.at[k, pl.ds(far + 4, 4)], xrr.at[k], at_x(3))
+        relay_l = send(ys.at[k, pl.ds(far, 4)], xrl.at[k], at_a(1))
+        relay_r = send(ys.at[k, pl.ds(far + 4, 4)], xrr.at[k], at_a(3))
         rounded(nxt)
-        plain_l = send(ys.at[k, pl.ds(nxt + 4, 4)], xinl.at[k, pl.ds(4, 4)], at_x(1))
+        plain_l = send(ys.at[k, pl.ds(nxt + 4, 4)], xinl.at[k, pl.ds(4, 4)], at_a(1))
         rounded(prv)
-        plain_r = send(ys.at[k, pl.ds(prv, 4)], xinr.at[k, pl.ds(0, 4)], at_x(3))
+        plain_r = send(ys.at[k, pl.ds(prv, 4)], xinr.at[k, pl.ds(0, 4)], at_a(3))
 
         def kept(i):
-            yown[k, i] = segment(0, own + i)
+            yown[k, i] = segment(0, tile_of(own, i))
 
         loop(8, kept)
         yield
@@ -203,10 +209,10 @@
 
         relay_l.wait_recv()
         loop(4, passed_l)
-        sum_l = send(ys.at[k, pl.ds(nxt, 4)], xinl.at[k, pl.ds(0, 4)], at_x(1))
+        sum_l = send(ys.at[k, pl.ds(nxt, 4)], xinl.at[k, pl.ds(0, 4)], at_a(1))
         relay_r.wait_recv()
         loop(4, passed_r)
-        sum_r = send(ys.at[k, pl.ds(prv + 4, 4)], xinr.at[k, pl.ds(4, 4)], at_x(3))
+        sum_r = send(ys.at[k, pl.ds(prv + 4, 4)], xinr.at[k, pl.ds(4, 4)], at_a(3))
         yield
         for copy in (plain_l, plain_r, sum_l, sum_r):
             copy.wait_recv()
@@ -217,18 +223,18 @@
             zs[k, i] = total.astype(BF16)
 
         loop(8, summed)
-        far, nxt, prv, own = (2 * turn(zh, by) for by in (2, 1, 3, 0))
-        relay_l = send(zs.at[k, far], zrl.at[k], at_h(1))
-        relay_r = send(zs.at[k, far + 1], zrr.at[k], at_h(3))
-        plain_l = send(zs.at[k, nxt + 1], zinl.at[k, 1], at_h(1))
-        plain_r = send(zs.at[k, prv], zinr.at[k, 0], at_h(3))
+        far, nxt, prv, own = (2 * turn(spot_b, by) for by in (2, 1, 3, 0))
+        relay_l = send(zs.at[k, far], zrl.at[k], at_b(1))
+        relay_r = send(zs.at[k, far + 1], zrr.at[k], at_b(3))
+        plain_l = send(zs.at[k, nxt + 1], zinl.at[k, 1], at_b(1))
+        plain_r = send(zs.at[k, prv], zinr.at[k, 0], at_b(3))
         yield
         relay_l.wait_recv()
         zs[k, nxt] = (yown[k, nxt] + zrl[k].astype(F32)).astype(BF16)
-        sum_l = send(zs.at[k, nxt], zinl.at[k, 0], at_h(1))
+        sum_l = send(zs.at[k, nxt], zinl.at[k, 0], at_b(1))
         relay_r.wait_recv()
         zs[k, prv + 1] = (yown[k, prv + 1] + zrr[k].astype(F32)).astype(BF16)
-        sum_r = send(zs.at[k, prv + 1], zinr.at[k, 1], at_h(3))
+        sum_r = send(zs.at[k, prv + 1], zinr.at[k, 1], at_b(3))
         yield
         for copy in (plain_l, plain_r, sum_l, sum_r):
             copy.wait_recv()
@@ -237,43 +243,49 @@
             aggt[k, :, i * TILE : (i + 1) * TILE] = total.astype(BF16)
         yield
 
-    def gather_col(k):
-        def whole(by_x, by_h):
-            return gg[k].at[pl.ds(2 * (turn(x, by_x) * 4 + turn(zh, by_h)), 2)]
-
-        def half(by_h, i):
-            return gg[k].at[2 * (x * 4 + turn(zh, by_h)) + i]
+    def gather_col(k, x_first):
+        at_a, at_b = (at_x, at_h) if x_first else (at_h, at_x)
+
+        def first_tile(by_a, by_b):
+            by_x, by_h = (by_a, by_b) if x_first else (by_b, by_a)
+            return 2 * (turn(x, by_x) * 4 + turn(zh, by_h))
+
+        def whole(by_a, by_b):
+            return gg[k].at[pl.ds(first_tile(by_a, by_b), 2)]
+
+        def half(by_a, i):
+            return gg[k].at[first_tile(by_a, 0) + i]
 
         right, left = {}, {}
 
-        def along_x(by_h):
-            right[by_h] = send(whole(0, by_h), whole(0, by_h), at_x(1))
-            left[by_h] = send(whole(0, by_h), whole(0, by_h), at_x(3))
-
-        up = send(whole(0, 0), whole(0, 0), at_h(1))
-        down = send(whole(0, 0), whole(0, 0), at_h(3))
-        yield
-        along_x(0)
+        def along_b(by_a):
+            right[by_a] = send(whole(by_a, 0), whole(by_a, 0), at_b(1))
+            left[by_a] = send(whole(by_a, 0), whole(by_a, 0), at_b(3))
+
+        up = send(whole(0, 0), whole(0, 0), at_a(1))
+        down = send(whole(0, 0), whole(0, 0), at_a(3))
+        yield
+        along_b(0)
         yield
         up.wait_recv()
-        relay_up = send(half(3, 0), half(3, 0), at_h(1))
-        along_x(3)
+        relay_up = send(half(3, 0), half(3, 0), at_a(1))
+        along_b(3)
         down.wait_recv()
-        relay_down = send(half(1, 1), half(1, 1), at_h(3))
-        along_x(1)
+        relay_down = send(half(1, 1), half(1, 1), at_a(3))
+        along_b(1)
         yield
         relay_up.wait_recv()
         relay_down.wait_recv()
-        along_x(2)
+        along_b(2)
         yield
         relays = []
-        for by_h in (0, 3, 1, 2):
-            right[by_h].wait_recv()
-            if by_h in (0, 1):
-                relays.append(send(whole(3, by_h), whole(3, by_h), at_x(1)))
-            left[by_h].wait_recv()
-            if by_h in (2, 3):
-                relays.append(send(whole(1, by_h), whole(1, by_h), at_x(3)))
+        for by_a in (0, 3, 1, 2):
+            right[by_a].wait_recv()
+            if by_a in (0, 1):
+                relays.append(send(whole(by_a, 3), whole(by_a, 3), at_b(1)))
+            left[by_a].wait_recv()
+            if by_a in (2, 3):
+                relays.append(send(whole(by_a, 1), whole(by_a, 1), at_b(3)))
         yield
         for copy in relays:
             copy.wait_recv()
@@ -357,31 +369,33 @@
         yield
 
     def reduce_weight():
-        rows_y = pl.multiple_of(32 * y, 32)
-        rows_x = pl.multiple_of(rows_y + 8 * x, 8)
+        rows_y = pl.multiple_of(64 * (y % 2), 64)
+        half_y = y // 2
+        rows_z = pl.multiple_of(rows_y + 32 * zl, 32)
+        rows_x = pl.multiple_of(rows_z + 8 * x, 8)
         lanes = pl.multiple_of(128 * zh, 128)
+
+        def y_part(buffer, by):
+            there = turn(y, by)
+            return buffer.at[core, there // 2, pl.ds(pl.multiple_of(64 * (there % 2), 64), 64)]
+
         copy = send(gsum.at[1 - core], rin_c, at_core)
         yield
         copy.wait_recv()
         gsum[core] += rin_c[...]
-        copy = send(gsum.at[core, 1 - zl], rin_z, at_z)
+        copies = [send(y_part(gsum, by), rin_y.at[by - 1], at_y(by)) for by in (1, 2, 3)]
+        yield
+        for copy in copies:
+            copy.wait_recv()
+        gsum[core, half_y, pl.ds(rows_y, 64)] += rin_y[0] + rin_y[1] + rin_y[2]
+        across_z = pl.ds(pl.multiple_of(rows_y + 32 - 32 * zl, 32), 32)
+        copy = send(gsum.at[core, half_y, across_z], rin_z, at_z)
         yield
         copy.wait_recv()
-        gsum[core, zl] += rin_z[...]
+        gsum[core, half_y, pl.ds(rows_z, 32)] += rin_z[...]
         copies = [
             send(
-                gsum.at[core, zl, pl.ds(pl.multiple_of(32 * turn(y, by), 32), 32)],
-                rin_y.at[by - 1], at_y(by),
-            )
-            for by in (1, 2, 3)
-        ]
-        yield
-        for copy in copies:
-            copy.wait_recv()
-        gsum[core, zl, pl.ds(rows_y, 32)] += rin_y[0] + rin_y[1] + rin_y[2]
-        copies = [
-            send(
-                gsum.at[core, zl, pl.ds(pl.multiple_of(rows_y + 8 * turn(x, by), 8), 8)],
+                gsum.at[core, half_y, pl.ds(pl.multiple_of(rows_z + 8 * turn(x, by), 8), 8)],
                 rin_x.at[by - 1], at_x(by),
             )
             for by in (1, 2, 3)
@@ -389,10 +403,10 @@
         yield
         for copy in copies:
             copy.wait_recv()
-        gsum[core, zl, pl.ds(rows_x, 8)] += rin_x[0] + rin_x[1] + rin_x[2]
+        gsum[core, half_y, pl.ds(rows_x, 8)] += rin_x[0] + rin_x[1] + rin_x[2]
         copies = [
             send(
-                gsum.at[core, zl, pl.ds(rows_x, 8), pl.ds(pl.multiple_of(128 * turn(zh, by), 128), 128)],
+                gsum.at[core, half_y, pl.ds(rows_x, 8), pl.ds(pl.multiple_of(128 * turn(zh, by), 128), 128)],
                 rin_h.at[by - 1], at_h(by),
             )
             for by in (1, 2, 3)
@@ -400,13 +414,13 @@
         yield
         for copy in copies:
             copy.wait_recv()
-        corner = (core, zl, pl.ds(rows_x, 8), pl.ds(lanes, 128))
+        corner = (core, half_y, pl.ds(rows_x, 8), pl.ds(lanes, 128))
         gout[corner] = gsum[corner] + rin_h[0] + rin_h[1] + rin_h[2]
         for cut, where in (
             (corner, [at_h(by) for by in (1, 2, 3)]),
-            ((core, zl, pl.ds(rows_x, 8)), [at_x(by) for by in (1, 2, 3)]),
-            ((core, zl, pl.ds(rows_y, 32)), [at_y(by) for by in (1, 2, 3)]),
-            ((core, zl), [at_z]),
+            ((core, half_y, pl.ds(rows_x, 8)), [at_x(by) for by in (1, 2, 3)]),
+            ((core, half_y, pl.ds(rows_z, 32)), [at_z]),
+            ((core, half_y, pl.ds(rows_y, 64)), [at_y(by) for by in (1, 2, 3)]),
             ((core,), [at_core]),
         ):
             copies = [send(gout.at[cut], gout.at[cut], peer) for peer in where]
@@ -423,7 +437,7 @@
             next(gen)
 
     rows = [gather_row(k) for k in range(2)]
-    cols = [reduce_col(q) for q in range(4)]
+    cols = [reduce_col(q, q == 1) for q in range(4)]
     go(rows[0])
     drawn[...] = jnp.zeros((8, TILE), jnp.int32)
     drawn[0:2, 0:SLOTS] = coords[...]
@@ -442,29 +456,28 @@
     go(cols[0], 2)
     go(rows[1])
     go(rows[0])
+    go(cols[1], 2)
+    go(rows[1])
+    go(cols[0])
+    go(rows[1])
+    go(cols[2], 2)
+    go(cols[0])
+    go(rows[1])
+    go(cols[3], 2)
+    go(cols[2])
     go(cols[1])
     go(cols[0])
-    go(cols[1])
-    go(rows[1], 2)
-    go(cols[2])
-    go(cols[1])
-    go(cols[2])
-    go(cols[0])
-    go(rows[1])
-    go(cols[3])
     go(cols[2])
     go(cols[3])
     go(cols[0])
     go(cols[1])
-    go(cols[0])
+    go(cols[2])
     go(cols[3])
     go(cols[1])
     go(cols[2])
+    go(cols[3])
     go(cols[1])
-    go(cols[2])
     go(cols[3])
-    go(cols[2])
-    go(cols[3], 2)
 
     def core_of(q):
         return core if q % 2 == 0 else 1 - core
@@ -485,7 +498,7 @@
             gg[q][2 * c + i] = part[:, i * TILE : (i + 1) * TILE]
 
     a, b, d, e = 1, 0, 3, 2
-    cols = [gather_col(q) for q in range(4)]
+    cols = [gather_col(q, False) for q in range(4)]
     rows = [reduce_row(k) for k in range(2)]
     total = reduce_weight()
     grad_agg(a)
@@ -590,8 +603,8 @@
             pltpu.VMEM((2, 2, 128, WIDTH), F32),
             pltpu.VMEM((2, 2, 128, WIDTH), F32),
             pltpu.VMEM((2, 128, WIDTH), F32),
-            pltpu.VMEM((128, WIDTH), F32),
-            pltpu.VMEM((3, 32, WIDTH), F32),
+            pltpu.VMEM((32, WIDTH), F32),
+            pltpu.VMEM((3, 64, WIDTH), F32),
             pltpu.VMEM((3, 8, WIDTH), F32),
             pltpu.VMEM((3, 8, 128), F32),
             pltpu.VMEM((SLOTS, TILE, TILE), BF16),

time: 154 us -> 147 us (0.955); the launches traced: 151 us -> 147 us
  Pallas kernels: 150 us -> 145 us
    pallas_call x1, Pallas kernels: 147 us -> 143 us  [body(): pl.pallas_call(kernel, out_shape=shapes, in_specs=[smem, vmem, vmem, hbm,...]
where the time goes in v3:
time: 147 us
  Pallas kernels  145 us (99%)
    pallas_call x1, Pallas kernels, body(): pl.pallas_call(kernel, out_shape=shapes, in_specs=[smem, vmem, vmem, hbm,...  143 us

profile of v3, /device:TPU:2, one launch (start us, length us, event | category | flops | bytes accessed | tf_op | source)
XLA Modules:
  0.0 146.5 jit_solution(13712041186680370788)
XLA Ops:
  1.3 142.7 %shard_map.85 = (bf16[256,512]{1,0:T(8,128)(2,1)}, f32[8,2,2,16,512]{4,3,2,1,0:T(8,128)}, bf16[32,4096]{1,0:T(8,128)(2,1)}) custom-call(s32[1,1]{1,0:T(1,128)S(6)} %copy.9.count, s32[2,96]{1,0:T(2,128)} %bitcast.11, bf16[32,4096]{1,0:T(8,128)(2,1)} %bitcast.10, bf16[96,128,128]{2,1,0:T(8,128)(2,1)} %bitcast.8, bf16[8,2,2,16,512]{4,3,2,1,0:T(8,128)(2,1)} %bitcast.9, ...), custom_call_target="tpu_custom_call" | custom-call | tf_op jit(solution)/shard_map/pallas_call | solution.py:571
  144.0 2.5 %shard_map.86 = (bf16[256,512]{1,0:T(8,128)(2,1)}, f32[8,2,2,16,512]{4,3,2,1,0:T(8,128)}, bf16[32,4096]{1,0:T(8,128)(2,1)}) custom-call(bf16[256,512]{1,0:T(8,128)(2,1)} %get-tuple-element.9.refs_0_, f32[8,2,2,16,512]{4,3,2,1,0:T(8,128)} %get-tuple-element.10.refs_1_, bf16[32,4096]{1,0:T(8,128)(2,1)} %get-tuple-element.11.refs_2_), custom_call_target="tpu_custom_call" | custom-call | tf_op jit(solution)/shard_map/pallas_call | solution.py:631

commit v4 on v3

--- a/solution.py
+++ b/solution.py
@@ -16,7 +16,7 @@
 CHUNK = 128
 NODES = 256
 UNROLL = 8
-WIRES = 192
+WIRES = 208
 
 NT = (((1,), (1,)), ((), ()))
 NN = (((1,), (0,)), ((), ()))
@@ -49,7 +49,7 @@
 def kernel(
     count, coords, xin, tiles_hbm, weight_hbm, cot_hbm, hid, gw, gft,
     xg0, xg1, xg2, xg3, run, ys, yown, xrl, xrr, xinl, xinr, zs, zrl, zrr, zinl, zinr,
-    aggt, gpre, gg0, gg1, gg2, gg3, bown, bsend, cin, yb, yrl, yrr, yinl, yinr, zout, zpin,
+    aggt, acted, gpre, gg0, gg1, gg2, gg3, bown, bsend, cin, yb, yrl, yrr, yinl, yinr, zout, zpin,
     gsum, gout, rin_c, rin_z, rin_y, rin_x, rin_h, tiles, weight, cot, drawn, made, table,
     send_sem, recv_sem, local_sem,
 ):
@@ -126,25 +126,36 @@
         def pass_on(owner):
             inside.append(send(own.at[owner], across.at[owner], at_core))
 
-        to_z = send(own.at[place], own.at[place], at_z)
-        up = send(own.at[place], own.at[place], at_y(1))
-        down = send(own.at[place], own.at[place], at_y(3))
+        def cross(owner, h, peer):
+            return send(part(owner, h), part(owner, h), peer)
+
+        to_z = [cross(place, h, at_z) for h in range(2)]
+        up = [cross(place, 0, at_y(1)), None]
+        down = [None, cross(place, 1, at_y(3))]
+        up[1] = cross(place, 1, at_y(1))
+        down[0] = cross(place, 0, at_y(3))
         pass_on(place)
         yield
-        to_z.wait_recv()
-        up_z = send(own.at[place_z], own.at[place_z], at_y(1))
-        down_z = send(own.at[place_z], own.at[place_z], at_y(3))
+        to_z[0].wait_recv()
+        up_z = [cross(place_z, 0, at_y(1)), None]
+        to_z[1].wait_recv()
+        down_z = [None, cross(place_z, 1, at_y(3))]
+        up_z[1] = cross(place_z, 1, at_y(1))
+        down_z[0] = cross(place_z, 0, at_y(3))
         pass_on(place_z)
         yield
         relays = []
-        for copy, by, side in ((up, 3, zl), (down, 1, zl), (up_z, 3, 1 - zl), (down_z, 1, 1 - zl)):
-            owner = 2 * turn(y, by) + side
-            copy.wait_recv()
-            if by == 3:
-                relays.append(send(part(owner, 0), part(owner, 0), at_y(1)))
-            else:
-                relays.append(send(part(owner, 1), part(owner, 1), at_y(3)))
-            pass_on(owner)
+        for ups, downs, side in ((up, down, zl), (up_z, down_z, 1 - zl)):
+            below, above = 2 * turn(y, 3) + side, 2 * turn(y, 1) + side
+            ups[0].wait_recv()
+            relays.append(cross(below, 0, at_y(1)))
+            downs[1].wait_recv()
+            relays.append(cross(above, 1, at_y(3)))
+        for ups, downs, side in ((up, down, zl), (up_z, down_z, 1 - zl)):
+            ups[1].wait_recv()
+            pass_on(2 * turn(y, 3) + side)
+            downs[0].wait_recv()
+            pass_on(2 * turn(y, 1) + side)
         yield
         for side, pair in ((zl, relays[:2]), (1 - zl, relays[2:])):
             for copy in pair:
@@ -436,6 +447,12 @@
         for _ in range(times):
             next(gen)
 
+    def core_of(q):
+        return core if q % 2 == 0 else 1 - core
+
+    def applied(q, cut):
+        return dot(aggt[q], weight[:, core_of(q), q // 2, :, cut].reshape(CHUNK, NODES), TN)
+
     rows = [gather_row(k) for k in range(2)]
     cols = [reduce_col(q, q == 1) for q in range(4)]
     go(rows[0])
@@ -467,26 +484,24 @@
     go(cols[2])
     go(cols[1])
     go(cols[0])
+    go(cols[0])
     go(cols[2])
-    go(cols[3])
-    go(cols[0])
-    go(cols[1])
-    go(cols[2])
-    go(cols[3])
-    go(cols[1])
-    go(cols[2])
-    go(cols[3])
     go(cols[1])
     go(cols[3])
-
-    def core_of(q):
-        return core if q % 2 == 0 else 1 - core
-
+    go(cols[2])
+    go(cols[1])
+    go(cols[3])
+    go(cols[2])
+    go(cols[1])
+    go(cols[3])
     for n in range(2):
         cut = slice(n * NODES, (n + 1) * NODES)
-        pre = jnp.zeros((NODES, NODES), F32)
-        for q in range(4):
-            pre += dot(aggt[q], weight[:, core_of(q), q // 2, :, cut].reshape(CHUNK, NODES), TN)
+        acted[:, cut] = applied(0, cut) + applied(1, cut) + applied(2, cut)
+    go(cols[3])
+
+    for n in range(2):
+        cut = slice(n * NODES, (n + 1) * NODES)
+        pre = acted[:, cut] + applied(3, cut)
         low = jnp.exp(jnp.minimum(pre, 0.0))
         hid[:, cut] = jnp.where(pre > 0, pre, low - 1.0).astype(BF16)
         slope = jnp.where(pre > 0, 1.0, low)
@@ -516,11 +531,11 @@
     go(cols[a])
     go(cols[d], 3)
     go(total)
+    go(cols[a])
+    go(rows[0])
     go(cols[b])
     go(cols[d])
     go(total)
-    go(cols[a])
-    go(rows[0])
     go(cols[e], 3)
     go(cols[d])
     go(cols[e])
@@ -588,6 +603,7 @@
             pltpu.VMEM((4, 2) + slab, BF16),
             pltpu.VMEM((4, 2) + slab, BF16),
             pltpu.VMEM((4, CHUNK, NODES), BF16),
+            pltpu.VMEM((NODES, WIDTH), F32),
             pltpu.VMEM((NODES, WIDTH), BF16),
             *[pltpu.VMEM((TILES,) + slab, BF16)] * 4,
             pltpu.VMEM((2, 8) + bits, F32),

time: 147 us -> 145 us (0.986)
  Pallas kernels: 145 us -> 143 us
    pallas_call x1, Pallas kernels: 143 us -> 141 us  [body(): pl.pallas_call(kernel, out_shape=shapes, in_specs=[smem, vmem, vmem, hbm,...]
where the time goes in v4:
time: 145 us
  Pallas kernels  143 us (99%)
    pallas_call x1, Pallas kernels, body(): pl.pallas_call(kernel, out_shape=shapes, in_specs=[smem, vmem, vmem, hbm,...  141 us

profile of v4, /device:TPU:2, one launch (start us, length us, event | category | flops | bytes accessed | tf_op | source)
XLA Modules:
  0.0 144.8 jit_solution(14408206873038950367)
XLA Ops:
  1.3 141.0 %shard_map.85 = (bf16[256,512]{1,0:T(8,128)(2,1)}, f32[8,2,2,16,512]{4,3,2,1,0:T(8,128)}, bf16[32,4096]{1,0:T(8,128)(2,1)}) custom-call(s32[1,1]{1,0:T(1,128)S(6)} %copy.9.count, s32[2,96]{1,0:T(2,128)} %bitcast.11, bf16[32,4096]{1,0:T(8,128)(2,1)} %bitcast.10, bf16[96,128,128]{2,1,0:T(8,128)(2,1)} %bitcast.8, bf16[8,2,2,16,512]{4,3,2,1,0:T(8,128)(2,1)} %bitcast.9, ...), custom_call_target="tpu_custom_call" | custom-call | tf_op jit(solution)/shard_map/pallas_call | solution.py:586
  142.3 2.5 %shard_map.86 = (bf16[256,512]{1,0:T(8,128)(2,1)}, f32[8,2,2,16,512]{4,3,2,1,0:T(8,128)}, bf16[32,4096]{1,0:T(8,128)(2,1)}) custom-call(bf16[256,512]{1,0:T(8,128)(2,1)} %get-tuple-element.9.refs_0_, f32[8,2,2,16,512]{4,3,2,1,0:T(8,128)} %get-tuple-element.10.refs_1_, bf16[32,4096]{1,0:T(8,128)(2,1)} %get-tuple-element.11.refs_2_), custom_call_target="tpu_custom_call" | custom-call | tf_op jit(solution)/shard_map/pallas_call | solution.py:647

commit v5 on v4

--- a/solution.py
+++ b/solution.py
@@ -329,10 +329,15 @@
 
                 loop(4, rows)
 
+        def half(h):
+            return pl.ds(16 * h, 16)
+
         inside[0].wait_recv()
         joined(far)
-        relay_l = send(yb.at[k, far], yrl.at[k], at_y(1))
-        relay_r = send(yb.at[k, far + 1], yrr.at[k], at_y(3))
+        relay_l, relay_r = [], []
+        for h in range(2):
+            relay_l.append(send(yb.at[k, far, half(h)], yrl.at[k, half(h)], at_y(1)))
+            relay_r.append(send(yb.at[k, far + 1, half(h)], yrr.at[k, half(h)], at_y(3)))
         inside[1].wait_recv()
         joined(nxt)
         plain_l = send(yb.at[k, nxt + 1], yinl.at[k, 1], at_y(1))
@@ -343,34 +348,42 @@
         joined(own)
         yield
 
-        def passed(at, came):
-            def rows(h):
-                cut = pl.ds(h * 8, 8)
+        def passed(at, came, h):
+            def rows(g):
+                cut = pl.ds(16 * h + g * 8, 8)
                 yb[k, at, cut] = (bown[k, at, cut] + came[k, cut].astype(F32)).astype(BF16)
 
-            loop(4, rows)
-
-        relay_l.wait_recv()
-        passed(nxt, yrl)
-        sum_l = send(yb.at[k, nxt], yinl.at[k, 0], at_y(1))
-        relay_r.wait_recv()
-        passed(prv + 1, yrr)
-        sum_r = send(yb.at[k, prv + 1], yinr.at[k, 1], at_y(3))
-        yield
-        for copy in (plain_l, plain_r, sum_l, sum_r):
-            copy.wait_recv()
+            loop(2, rows)
+
+        sum_l, sum_r = [], []
+        for h in range(2):
+            relay_l[h].wait_recv()
+            passed(nxt, yrl, h)
+            sum_l.append(send(yb.at[k, nxt, half(h)], yinl.at[k, 0, half(h)], at_y(1)))
+            relay_r[h].wait_recv()
+            passed(prv + 1, yrr, h)
+            sum_r.append(send(yb.at[k, prv + 1, half(h)], yinr.at[k, 1, half(h)], at_y(3)))
+        yield
+        plain_l.wait_recv()
+        plain_r.wait_recv()
 
         def total_of(i, cut):
             return bown[k, own + i, cut] + yinl[k, i, cut].astype(F32) + yinr[k, i, cut].astype(F32)
 
-        def leaving(h):
-            cut = pl.ds(h * 8, 8)
-            zout[k, cut] = total_of(1 - zl, cut).astype(BF16)
-
-        loop(4, leaving)
-        to_z = send(zout.at[k], zpin.at[k], at_z)
-        yield
-        to_z.wait_recv()
+        to_z = []
+        for h in range(2):
+            sum_l[h].wait_recv()
+            sum_r[h].wait_recv()
+
+            def leaving(g):
+                cut = pl.ds(16 * h + g * 8, 8)
+                zout[k, cut] = total_of(1 - zl, cut).astype(BF16)
+
+            loop(2, leaving)
+            to_z.append(send(zout.at[k, half(h)], zpin.at[k, half(h)], at_z))
+        yield
+        for copy in to_z:
+            copy.wait_recv()
 
         def final(s):
             cut = pl.ds(pl.multiple_of(s * TILE, TILE), TILE)
@@ -384,7 +397,6 @@
         half_y = y // 2
         rows_z = pl.multiple_of(rows_y + 32 * zl, 32)
         rows_x = pl.multiple_of(rows_z + 8 * x, 8)
-        lanes = pl.multiple_of(128 * zh, 128)
 
         def y_part(buffer, by):
             there = turn(y, by)
@@ -415,20 +427,13 @@
         for copy in copies:
             copy.wait_recv()
         gsum[core, half_y, pl.ds(rows_x, 8)] += rin_x[0] + rin_x[1] + rin_x[2]
-        copies = [
-            send(
-                gsum.at[core, half_y, pl.ds(rows_x, 8), pl.ds(pl.multiple_of(128 * turn(zh, by), 128), 128)],
-                rin_h.at[by - 1], at_h(by),
-            )
-            for by in (1, 2, 3)
-        ]
+        rin_h[zh] = gsum[core, half_y, pl.ds(rows_x, 8)]
+        copies = [send(rin_h.at[zh], rin_h.at[zh], at_h(by)) for by in (1, 2, 3)]
         yield
         for copy in copies:
             copy.wait_recv()
-        corner = (core, half_y, pl.ds(rows_x, 8), pl.ds(lanes, 128))
-        gout[corner] = gsum[corner] + rin_h[0] + rin_h[1] + rin_h[2]
+        gout[core, half_y, pl.ds(rows_x, 8)] = (rin_h[0] + rin_h[1]) + (rin_h[2] + rin_h[3])
         for cut, where in (
-            (corner, [at_h(by) for by in (1, 2, 3)]),
             ((core, half_y, pl.ds(rows_x, 8)), [at_x(by) for by in (1, 2, 3)]),
             ((core, half_y, pl.ds(rows_z, 32)), [at_z]),
             ((core, half_y, pl.ds(rows_y, 64)), [at_y(by) for by in (1, 2, 3)]),
@@ -557,7 +562,6 @@
     go(total)
     go(rows[0])
     go(rows[1])
-    go(total)
     go(rows[1])
     for copy in started:
         copy.wait_send()
@@ -622,7 +626,7 @@
             pltpu.VMEM((32, WIDTH), F32),
             pltpu.VMEM((3, 64, WIDTH), F32),
             pltpu.VMEM((3, 8, WIDTH), F32),
-            pltpu.VMEM((3, 8, 128), F32),
+            pltpu.VMEM((4, 8, WIDTH), F32),
             pltpu.VMEM((SLOTS, TILE, TILE), BF16),
             pltpu.VMEM((8, 2, 2, 16, WIDTH), BF16),
             pltpu.VMEM((NODES, WIDTH), BF16),

time: 145 us -> 142 us (0.979)
  Pallas kernels: 143 us -> 139 us
    pallas_call x1, Pallas kernels: 141 us -> 137 us  [body(): pl.pallas_call(kernel, out_shape=shapes, in_specs=[smem, vmem, vmem, hbm,...]
where the time goes in v5:
time: 142 us; the launch traced here: 141 us
  Pallas kernels  139 us (98%)
    pallas_call x1, Pallas kernels, body(): pl.pallas_call(kernel, out_shape=shapes, in_specs=[smem, vmem, vmem, hbm,...  137 us

profile of v5, /device:TPU:2, one launch (start us, length us, event | category | flops | bytes accessed | tf_op | source)
XLA Modules:
  0.0 140.7 jit_solution(17049572493055012314)
XLA Ops:
  1.3 136.9 %shard_map.85 = (bf16[256,512]{1,0:T(8,128)(2,1)}, f32[8,2,2,16,512]{4,3,2,1,0:T(8,128)}, bf16[32,4096]{1,0:T(8,128)(2,1)}) custom-call(s32[1,1]{1,0:T(1,128)S(6)} %copy.9.count, s32[2,96]{1,0:T(2,128)} %bitcast.11, bf16[32,4096]{1,0:T(8,128)(2,1)} %bitcast.10, bf16[96,128,128]{2,1,0:T(8,128)(2,1)} %bitcast.8, bf16[8,2,2,16,512]{4,3,2,1,0:T(8,128)(2,1)} %bitcast.9, ...), custom_call_target="tpu_custom_call" | custom-call | tf_op jit(solution)/shard_map/pallas_call | solution.py:590
  138.2 2.5 %shard_map.86 = (bf16[256,512]{1,0:T(8,128)(2,1)}, f32[8,2,2,16,512]{4,3,2,1,0:T(8,128)}, bf16[32,4096]{1,0:T(8,128)(2,1)}) custom-call(bf16[256,512]{1,0:T(8,128)(2,1)} %get-tuple-element.9.refs_0_, f32[8,2,2,16,512]{4,3,2,1,0:T(8,128)} %get-tuple-element.10.refs_1_, bf16[32,4096]{1,0:T(8,128)(2,1)} %get-tuple-element.11.refs_2_), custom_call_target="tpu_custom_call" | custom-call | tf_op jit(solution)/shard_map/pallas_call | solution.py:651
